TPU v7x, 512 devices: a whole 4x4x16 slice. The times are simulated.
512 devices in a mesh: row: 32 (over z, core), col: 16 (over x, y).
Axes of the slice: x: 4, y: 4, z: 16, core: 2. Of those that a mesh axis runs over, the one named last changes fastest.
Arguments:
- tokens: bfloat16 [262144, 1024], P(('row', 'col')), may hold values from -64 to 64, as said below
- merge_map: int32 [262144], P(('row', 'col')), may hold values from 0 to 511, as said below
- block_owner: int32 [512, 8], P(('row', 'col')), may hold values from -1 to 63, as said below
- neighbours: int32 [1024, 16], P(('row', 'col')), may hold values from 0 to 31, as said below
- w_query: bfloat16 [1024, 512], replicated, may hold values from -0.1875 to 0.1875
- w_key: bfloat16 [1024, 512], replicated, may hold values from -0.1875 to 0.1875
- w_value: bfloat16 [1024, 512], replicated, may hold values from -0.1875 to 0.1875
Outputs:
- attended: bfloat16 [262144, 512], P(('row', 'col'))
Inputs may be any that keep to these rules, and one draw needn't show every extreme that they name: `merge_map`: within a tile, the slots of its live blocks (those whose block_owner is not -1) are each used by one or more tokens, and no other slot is used. `block_owner`: A tile's live blocks are its first ones, 1 to 8 of them, 8 in some tile of every column index; a code o names owned block o % 2 of the device with row index o // 2 and the tile's column index; within one column index every code is named exactly once; one tile names each row index at most once. `neighbours`: the entries of a row are distinct, and the first is the block's own candidate number. `tokens`: finite bfloat16 values.
All inputs are finite; a program needn't handle non-finite values.
Results may differ from a plain program's by a relative error of at most 0.019.
The roundings to bfloat16 on the way count: a program that leaves them out, or rounds other values in their place, can miss the bound.
Values may be sent and summed in bfloat16 or wider, within the bound.
A program may use at most 64 MiB of HBM per device.

v0:
```python
import math

import jax
import jax.numpy as jnp
from jax import lax
from jax.sharding import PartitionSpec as P

D = 1024
HEADS = 8
HD = 64
BLK = 64
OWN = 2
SLOTS_BLK = 8


def on_device(tokens, merge_map, block_owner, neighbours, w_query, w_key, w_value):
    row_count = lax.axis_size("row")
    col_count = lax.axis_size("col")
    slot_total = SLOTS_BLK * BLK
    head_width = HEADS * HD
    cand_total = col_count * OWN
    query_count = OWN * BLK
    score_scale = 1.0 / math.sqrt(HD)
    slot_ids = lax.broadcasted_iota(jnp.int32, (slot_total, tokens.shape[0]), 0)
    onehot = (slot_ids == merge_map[None, :]).astype(jnp.bfloat16)
    slot_sums = jnp.dot(onehot, tokens, preferred_element_type=jnp.float32)
    slot_count = jnp.sum(onehot.astype(jnp.float32), axis=1)
    merged = (slot_sums / jnp.maximum(slot_count, 1.0)[:, None]).astype(jnp.bfloat16)
    dest_code = block_owner[0]
    dest_row = dest_code // OWN
    merged_blocks = merged.reshape(SLOTS_BLK, BLK * D)
    peer_ids = lax.broadcasted_iota(jnp.int32, (row_count, SLOTS_BLK), 0)
    select = (peer_ids == dest_row[None, :]) & (dest_code[None, :] >= 0)
    outgoing = jnp.dot(
        select.astype(jnp.bfloat16), merged_blocks, preferred_element_type=jnp.float32
    )
    outgoing = outgoing.astype(jnp.bfloat16).reshape(row_count, BLK, D)
    slot_tag = jnp.sum(jnp.where(select, dest_code[None, :] % OWN + 1, 0), axis=1) - 1
    arrived, arrived_tag = (
        lax.all_to_all(outgoing, "row", split_axis=0, concat_axis=0, tiled=True),
        lax.all_to_all(slot_tag, "row", split_axis=0, concat_axis=0, tiled=True),
    )
    own_ids = lax.broadcasted_iota(jnp.int32, (OWN, row_count), 0)
    place_map = (own_ids == arrived_tag[None, :]).astype(jnp.bfloat16)
    owned_tokens = jnp.dot(
        place_map, arrived.reshape(row_count, BLK * D), preferred_element_type=jnp.float32
    )
    owned_tokens = owned_tokens.astype(jnp.bfloat16).reshape(query_count, D)
    query_rows = jnp.dot(owned_tokens, w_query, preferred_element_type=jnp.float32).astype(
        jnp.bfloat16
    )
    query_heads = query_rows.reshape(query_count, HEADS, HD)
    cand_ids = lax.broadcasted_iota(jnp.int32, (1, 1, cand_total), 2)
    allowed = jnp.any(neighbours[:, :, None] == cand_ids, axis=1).astype(jnp.float32)
    token_piece = lax.all_gather(owned_tokens, "col", axis=0, tiled=True)
    key_rows = jnp.dot(token_piece, w_key, preferred_element_type=jnp.float32).astype(jnp.bfloat16)
    value_rows = jnp.dot(token_piece, w_value, preferred_element_type=jnp.float32).astype(
        jnp.bfloat16
    )
    run_max = jnp.full((HEADS, query_count), -1e30, jnp.float32)
    key_count = key_rows.shape[0]
    key_heads = key_rows.reshape(key_count, HEADS, HD)
    value_heads = value_rows.reshape(key_count, HEADS, HD)
    scores = (
        jnp.einsum("qhd,khd->hqk", query_heads, key_heads, preferred_element_type=jnp.float32)
        * score_scale
    )
    key_block = lax.broadcasted_iota(jnp.int32, (key_count, cand_total), 0) // BLK
    block_hit = (key_block == lax.broadcasted_iota(jnp.int32, (key_count, cand_total), 1)).astype(
        jnp.float32
    )
    visible = jnp.dot(allowed, block_hit.T) > 0.5
    visible = jnp.repeat(visible, BLK, axis=0)[None]
    scores = jnp.where(visible, scores, -1e30)
    new_max = jnp.maximum(run_max, jnp.max(scores, axis=-1))
    probs = jnp.where(visible, jnp.exp(scores - new_max[..., None]), 0.0)
    new_sum = jnp.sum(probs, axis=-1)
    product = jnp.einsum(
        "hqk,khd->hqd", probs.astype(jnp.bfloat16), value_heads, preferred_element_type=jnp.float32
    )
    final_state = (new_max, new_sum, product)
    run_max, run_sum, run_acc = final_state
    head_out = (
        (run_acc / run_sum[..., None])
        .transpose(1, 0, 2)
        .reshape(query_count, head_width)
        .astype(jnp.bfloat16)
    )
    reply_map = (
        lax.broadcasted_iota(jnp.int32, (row_count, OWN), 1) == arrived_tag[:, None]
    ).astype(jnp.bfloat16)
    replies = jnp.dot(
        reply_map, head_out.reshape(OWN, BLK * head_width), preferred_element_type=jnp.float32
    )
    replies = replies.astype(jnp.bfloat16).reshape(row_count, BLK, head_width)
    returned = lax.all_to_all(replies, "row", split_axis=0, concat_axis=0, tiled=True)
    returned_rows = returned.reshape(row_count * BLK, head_width)
    token_block = merge_map // BLK
    block_ids = lax.broadcasted_iota(jnp.int32, (1, SLOTS_BLK), 1)
    token_dest = jnp.sum(jnp.where(token_block[:, None] == block_ids, dest_row[None, :], 0), axis=1)
    token_index = token_dest * BLK + merge_map % BLK
    return jnp.take(returned_rows, token_index, axis=0)


def solution(mesh):
    in_specs = (
        P(("row", "col"), None),
        P(("row", "col")),
        P(("row", "col"), None),
        P(("row", "col"), None),
        P(),
        P(),
        P(),
    )
    out_specs = P(("row", "col"), None)
    return jax.shard_map(
        on_device, mesh=mesh, in_specs=in_specs, out_specs=out_specs, check_vma=False
    )
```

profile of v0, /device:TPU:1, one launch (start us, length us, event | category | flops | bytes accessed | tf_op | source)
XLA Modules:
  0.0 442.2 jit_solution(11282050828562101193)
XLA Ops:
  6.5 0.8 fusion.34
  7.3 0.7 compare_bitcast_fusion
  8.0 0.7 copy.17
  8.7 16.7 %all-to-all-start = ((s32[32,1,1]{2,1,0:T(1,128)}), s32[32,1,1]{2,1,0:T(1,128)S(1)}, u32[]{:S(2)}, u32[]{:S(2)}) async-start(s32[32,1,1]{2,1,0:T(1,128)} %copy.17), calls=%async_computation | async-start | bytes 32768 | tf_op jit(solution)/shard_map/all_to_all | solution.py:41
  25.5 0.9 convert_reduce_fusion
  26.4 2.0 divide_convert_fusion
  28.3 0.5 reshape.62
  28.8 1.4 convolution_convert_fusion
  30.2 4.3 copy.20
  34.5 2.7 all-to-all-done
  37.2 9.5 %all-to-all-start.1 = ((bf16[32,64,1024]{2,1,0:T(8,128)(2,1)}), bf16[32,64,1024]{2,1,0:T(8,128)(2,1)}, u32[]{:S(2)}, u32[]{:S(2)}) async-start(bf16[32,64,1024]{2,1,0:T(8,128)(2,1)} %bitcast.41), calls=%async_computation.1 | async-start | bytes 8388608 | tf_op jit(solution)/shard_map/all_to_all | solution.py:40
  46.8 0.7 reduce
  47.4 182.6 %all-to-all-done.1 = bf16[32,64,1024]{2,1,0:T(8,128)(2,1)} async-done(((bf16[32,64,1024]{2,1,0:T(8,128)(2,1)}), bf16[32,64,1024]{2,1,0:T(8,128)(2,1)}, u32[]{:S(2)}, u32[]{:S(2)}) %all-to-all-start.1) | async-done | bytes 4194336 | tf_op jit(solution)/shard_map/all_to_all | solution.py:40
  230.0 4.5 %copy.21 = bf16[4,8,64,1024]{3,1,2,0:T(8,128)(2,1)S(1)} copy(bf16[4,8,64,1024]{3,2,1,0:T(8,128)(2,1)} %bitcast.13) | data formatting | bytes 8388608
  234.5 0.7 convolution_convert_fusion.1
  235.2 0.9 reshape.65
  236.3 2.3 convolution_compare_fusion
  238.6 1.3 convolution_convert_fusion.5
  240.0 62.1 %all-gather.2.cloned.1.call-done = bf16[2048,1024]{1,0:T(8,128)(2,1)} async-done(((bf16[128,1024]{1,0:T(8,128)(2,1)}), bf16[2048,1024]{1,0:T(8,128)(2,1)}) %all-gather.2.cloned.1.call-update) | async-done | bytes 4194320 | tf_op jit(solution)/shard_map/all_gather | solution.py:55
  302.1 4.6 %convolution_convert_fusion.4 = bf16[2048,512]{0,1:T(8,128)(2,1)S(1)} fusion(bf16[2048,1024]{1,0:T(8,128)(2,1)} %all-gather.2.cloned.1.call-done, bf16[1024,512]{1,0:T(8,128)(2,1)S(1)} %copy-done), kind=kOutput, calls=%fused_computation.12 | convolution fusion | flops 2148532224 | bytes 7340032 | tf_op jit(solution)/shard_map/dot_general | solution.py:56
  306.7 1.7 fusion
  308.5 2.5 fusion.1
  311.0 2.4 convolution_convert_fusion.3
  313.4 2.4 fusion.12
  315.8 0.2 copy.19
  316.0 0.3 convert_element_type.52
  316.3 0.7 convolution_convert_fusion.2
  317.0 2.1 copy.22
  319.1 13.0 %all-to-all-start.2 = ((bf16[32,64,512]{2,1,0:T(8,128)(2,1)}), bf16[32,64,512]{2,1,0:T(8,128)(2,1)S(1)}, u32[]{:S(2)}, u32[]{:S(2)}) async-start(bf16[32,64,512]{2,1,0:T(8,128)(2,1)} %bitcast.44), calls=%async_computation.2 | async-start | bytes 4194304 | tf_op jit(solution)/shard_map/all_to_all | solution.py:96
  332.3 98.5 %all-to-all-done.2 = bf16[32,64,512]{2,1,0:T(8,128)(2,1)S(1)} async-done(((bf16[32,64,512]{2,1,0:T(8,128)(2,1)}), bf16[32,64,512]{2,1,0:T(8,128)(2,1)S(1)}, u32[]{:S(2)}, u32[]{:S(2)}) %all-to-all-start.2) | async-done | bytes 2097184 | tf_op jit(solution)/shard_map/all_to_all | solution.py:96
  430.7 2.6 gather_fusion
  433.4 2.0 broadcast_select_fusion
  (27 shorter events, 0.6 us)
Async XLA Ops:
  6.5 295.5 %copy-start = (bf16[1024,512]{1,0:T(8,128)(2,1)S(1)}, bf16[1024,512]{1,0:T(8,128)(2,1)}, u32[]{:S(2)}) copy-start(bf16[1024,512]{1,0:T(8,128)(2,1)} %param.12) | copy-start | bytes 3145732
  8.7 28.5 %all-to-all-start = ((s32[32,1,1]{2,1,0:T(1,128)}), s32[32,1,1]{2,1,0:T(1,128)S(1)}, u32[]{:S(2)}, u32[]{:S(2)}) async-start(s32[32,1,1]{2,1,0:T(1,128)} %copy.17), calls=%async_computation | async-start | bytes 32768 | tf_op jit(solution)/shard_map/all_to_all | solution.py:41
  37.2 192.8 %all-to-all-start.1 = ((bf16[32,64,1024]{2,1,0:T(8,128)(2,1)}), bf16[32,64,1024]{2,1,0:T(8,128)(2,1)}, u32[]{:S(2)}, u32[]{:S(2)}) async-start(bf16[32,64,1024]{2,1,0:T(8,128)(2,1)} %bitcast.41), calls=%async_computation.1 | async-start | bytes 8388608 | tf_op jit(solution)/shard_map/all_to_all | solution.py:40
  46.7 255.3 %all-gather.2.cloned.1.call-start = ((), (), s32[]{:S(2)}) async-start(), calls=%async_computation.3 | async-start | bytes 4456448 | tf_op jit(solution)/shard_map/all_gather | solution.py:55
  234.5 1.7 copy-start.5
  234.5 4.1 copy-start.1
  308.4 2.5 copy-start.3
  308.4 2.5 copy-start.4
  317.0 15.1 %copy-start.2 = (s32[512]{0:T(512)S(1)}, s32[512]{0:T(512)}, u32[]{:S(2)}) copy-start(s32[512]{0:T(512)} %param.8) | copy-start | bytes 6148
  319.1 111.6 %all-to-all-start.2 = ((bf16[32,64,512]{2,1,0:T(8,128)(2,1)}), bf16[32,64,512]{2,1,0:T(8,128)(2,1)S(1)}, u32[]{:S(2)}, u32[]{:S(2)}) async-start(bf16[32,64,512]{2,1,0:T(8,128)(2,1)} %bitcast.44), calls=%async_computation.2 | async-start | bytes 4194304 | tf_op jit(solution)/shard_map/all_to_all | solution.py:96
Sparse Core Ops, SparseCore 0:
  236.3 65.7 all-gather.1
where the time goes:
time: 443 us; the launch traced here: 442 us
  waiting for transfers between devices  346 us (78%)
  starting transfers between devices  39.3 us (9%)
  matrix products  19.4 us (4%)
  local copies, waits for them, and re-layouts  16.3 us (4%)
  between operations  13.6 us (3%)
  other arithmetic  7.74 us (2%)
    all_to_all x1, waiting for transfers between devices, on_device(): lax.all_to_all(outgoing, 'row', split_axis=0, concat_axis=0, tiled=True)  183 us
    all_to_all x1, waiting for transfers between devices, on_device(): lax.all_to_all(replies, 'row', split_axis=0, concat_axis=0, tiled=True)  98.5 us
    all_gather x1, waiting for transfers between devices, on_device(): token_piece = lax.all_gather(owned_tokens, 'col', axis=0, tiled=True)  62.1 us
    all_to_all x1, starting transfers between devices, on_device(): lax.all_to_all(slot_tag, 'row', split_axis=0, concat_axis=0, tiled=True)  16.7 us
    all_to_all x1, starting transfers between devices, on_device(): lax.all_to_all(replies, 'row', split_axis=0, concat_axis=0, tiled=True)  13 us
    unnamed x15, local copies, waits for them, and re-layouts  10.9 us
    all_to_all x1, starting transfers between devices, on_device(): lax.all_to_all(outgoing, 'row', split_axis=0, concat_axis=0, tiled=True)  9.51 us
  transfers between devices with their start and end apart: 4, of which 4 were waited for; matrix products, arithmetic and copies ran while one was open for 3% of the time, Pallas kernels for 0%

commit v1 on v0

v1 whole, which is shorter than its diff:
```python
import functools
import math

import jax
import jax.numpy as jnp
from jax import lax
from jax.experimental import pallas as pl
from jax.experimental.pallas import tpu as pltpu
from jax.sharding import PartitionSpec as P

HD = 64
BLK = 64
OWN = 2
SLOTS_BLK = 8
STEPS = 16
DELAY = 2
MESH = pl.DeviceIdType.MESH


def on_device(tokens, merge_map, block_owner, neighbours, w_query, w_key, w_value):
    row_count = lax.axis_size("row")
    col_count = lax.axis_size("col")
    slot_total = SLOTS_BLK * BLK
    width = tokens.shape[1]
    head_width = w_query.shape[1]
    heads = head_width // HD
    cand_total = col_count * OWN
    query_count = OWN * BLK
    score_scale = 1.0 / math.sqrt(HD)
    slot_ids = lax.broadcasted_iota(jnp.int32, (slot_total, tokens.shape[0]), 0)
    onehot = (slot_ids == merge_map[None, :]).astype(jnp.bfloat16)
    slot_sums = jnp.dot(onehot, tokens, preferred_element_type=jnp.float32)
    slot_count = jnp.sum(onehot.astype(jnp.float32), axis=1)
    merged = (slot_sums / jnp.maximum(slot_count, 1.0)[:, None]).astype(jnp.bfloat16)
    dest_code = block_owner[0]
    dest_row = dest_code // OWN
    merged_blocks = merged.reshape(SLOTS_BLK, BLK * width)
    peer_ids = lax.broadcasted_iota(jnp.int32, (row_count, SLOTS_BLK), 0)
    select = (peer_ids == dest_row[None, :]) & (dest_code[None, :] >= 0)
    outgoing = jnp.dot(
        select.astype(jnp.bfloat16), merged_blocks, preferred_element_type=jnp.float32
    )
    outgoing = outgoing.astype(jnp.bfloat16).reshape(row_count, BLK, width)
    slot_tag = jnp.sum(jnp.where(select, dest_code[None, :] % OWN + 1, 0), axis=1) - 1
    arrived = lax.all_to_all(outgoing, "row", split_axis=0, concat_axis=0, tiled=True)
    arrived_tag = lax.all_to_all(slot_tag, "row", split_axis=0, concat_axis=0, tiled=True)
    own_ids = lax.broadcasted_iota(jnp.int32, (OWN, row_count), 0)
    place_map = (own_ids == arrived_tag[None, :]).astype(jnp.bfloat16)
    owned_tokens = jnp.dot(
        place_map, arrived.reshape(row_count, BLK * width), preferred_element_type=jnp.float32
    )
    owned_tokens = owned_tokens.astype(jnp.bfloat16).reshape(query_count, width)
    query_rows = jnp.dot(owned_tokens, w_query, preferred_element_type=jnp.float32).astype(
        jnp.bfloat16
    )
    query_heads = query_rows.reshape(query_count, heads, HD)
    cand_ids = lax.broadcasted_iota(jnp.int32, (1, 1, cand_total), 2)
    allowed = jnp.any(neighbours[:, :, None] == cand_ids, axis=1)
    token_piece = lax.all_gather(owned_tokens, "col", axis=0, tiled=True)
    key_rows = jnp.dot(token_piece, w_key, preferred_element_type=jnp.float32).astype(jnp.bfloat16)
    value_rows = jnp.dot(token_piece, w_value, preferred_element_type=jnp.float32).astype(
        jnp.bfloat16
    )
    key_count = key_rows.shape[0]
    key_heads = key_rows.reshape(key_count, heads, HD)
    value_heads = value_rows.reshape(key_count, heads, HD)
    scores = (
        jnp.einsum("qhd,khd->hqk", query_heads, key_heads, preferred_element_type=jnp.float32)
        * score_scale
    )
    visible = jnp.repeat(jnp.repeat(allowed, BLK, axis=0), BLK, axis=1)[None]
    scores = jnp.where(visible, scores, -1e30)
    new_max = jnp.max(scores, axis=-1)
    probs = jnp.where(visible, jnp.exp(scores - new_max[..., None]), 0.0)
    new_sum = jnp.sum(probs, axis=-1)
    product = jnp.einsum(
        "hqk,khd->hqd", probs.astype(jnp.bfloat16), value_heads, preferred_element_type=jnp.float32
    )
    head_out = (
        (product / new_sum[..., None])
        .transpose(1, 0, 2)
        .reshape(query_count, head_width)
        .astype(jnp.bfloat16)
    )
    reply_map = (
        lax.broadcasted_iota(jnp.int32, (row_count, OWN), 1) == arrived_tag[:, None]
    ).astype(jnp.bfloat16)
    replies = jnp.dot(
        reply_map, head_out.reshape(OWN, BLK * head_width), preferred_element_type=jnp.float32
    )
    replies = replies.astype(jnp.bfloat16).reshape(row_count, BLK, head_width)
    returned = lax.all_to_all(replies, "row", split_axis=0, concat_axis=0, tiled=True)
    returned_rows = returned.reshape(row_count * BLK, head_width)
    token_block = merge_map // BLK
    block_ids = lax.broadcasted_iota(jnp.int32, (1, SLOTS_BLK), 1)
    token_dest = jnp.sum(jnp.where(token_block[:, None] == block_ids, dest_row[None, :], 0), axis=1)
    token_index = token_dest * BLK + merge_map % BLK
    return jnp.take(returned_rows, token_index, axis=0)


def plan_routes(rx_codes, tbl_v, nz, z, steps):
    shape = (max(nz, 8), 128)
    lane = lax.broadcasted_iota(jnp.int32, shape, 1)
    chip = lax.broadcasted_iota(jnp.int32, shape, 0)
    place = jnp.sum(rx_codes, axis=0)
    place = jnp.sum(place, axis=0, keepdims=True)
    place = jnp.broadcast_to(place, shape)
    valid = place > 0
    place = place - 1
    pos = jnp.where(valid, place >> 4, 0)
    loc = jnp.where(valid, place & 15, 0)
    fwd = ((lane >> 2) - pos) & (nz - 1)
    half = nz // 2
    right = (fwd < half) | ((fwd == half) & ((lane & 1) == 0))
    rem = jnp.where(valid, jnp.where(right, fwd, nz - fwd), 0)
    right_i = right.astype(jnp.int32)
    mine = chip == z
    back = jnp.full(shape, 2 * steps, jnp.int32)

    def step(t, state):
        pos, rem, ready, loc, send, back = state
        open_ = (rem > 0) & (ready <= t) & (pos == chip)
        key = rem * 128 + lane + 1
        for d in range(2):
            here = open_ & (right_i == 1 - d)
            keyed = jnp.where(here, key, 0)
            best = jnp.max(keyed, axis=1, keepdims=True)
            pick = jnp.where(here & (keyed == best), 1, 0)
            moved = jnp.broadcast_to(jnp.max(pick, axis=0, keepdims=True), shape) > 0
            own = jnp.sum(jnp.where(mine, pick * (loc + 1), 0), axis=1, keepdims=True)
            own = jnp.broadcast_to(jnp.sum(own, axis=0, keepdims=True), shape)
            slot = 2 * t + d
            send = jnp.where(lane == slot, jnp.maximum(own - 1, 0), send)
            back = jnp.where(lane == own - 1, slot, back)
            pos = jnp.where(moved, (pos + (1 - 2 * d)) & (nz - 1), pos)
            rem = jnp.where(moved, rem - 1, rem)
            ready = jnp.where(moved, t + DELAY, ready)
            loc = jnp.where(moved, 16 + slot, loc)
        return pos, rem, ready, loc, send, back

    zero = jnp.zeros(shape, jnp.int32)
    pos, rem, ready, loc, send, back = lax.fori_loop(
        0, steps, step, (pos, rem, zero, loc, zero, back)
    )
    final = zero
    for i in range(2 * OWN):
        at = jnp.sum(jnp.where(lane == 2 * OWN * z + i, loc, 0), axis=1, keepdims=True)
        at = jnp.broadcast_to(at, shape)
        back = jnp.where(lane == at, 2 * steps + i, back)
        final = jnp.where(lane == i, at, final)
    row8 = lax.broadcasted_iota(jnp.int32, (8, 128), 0)
    table = jnp.where(row8 == 0, send[:8], jnp.where(row8 == 1, back[:8], final[:8]))
    tbl_v[...] = table
    return jnp.broadcast_to(jnp.max(rem, axis=1, keepdims=True), shape)[:8]


def kernel(
    dims,
    tokens_hbm, map_ref, owner_ref, nb_ref, wq_hbm, wk_hbm, wv_hbm,
    out_ref, flag_ref,
    tok, wts, onehot, onehot_t,
    codes_tx, codes_rx, tbl_v, tbl_s,
    local, sib_tx, sib_rx, stage, recv, fin_tx, fin_rx, owned,
    msg_tx, msg_rx, pairs, nb_tx, nb_rx, nb_s,
    att_tx, att_rx, home, ret_stage, ret_recv, ret_tx, ret_rx,
    load_sem, codes_ssem, codes_rsem, pair_ssem, pair_rsem, hop_ssem, hop_rsem,
    msg_ssem, msg_rsem, nb_ssem, nb_rsem, att_ssem, att_rsem, ret_ssem, ret_rsem,
):
    nrow, ncol, heads, width, steps = dims
    nz = nrow // 2
    half = width // 2
    hh = heads // 2
    hw = hh * HD
    half_col = ncol // 2
    slots = SLOTS_BLK * BLK
    row = lax.axis_index("row")
    col = lax.axis_index("col")
    z = row // 2
    core = lax.rem(row, 2)
    sib = row + 1 - 2 * core
    barrier = pltpu.get_barrier_semaphore()

    loads = [pltpu.make_async_copy(tokens_hbm, tok, load_sem.at[0])]
    for i, w in enumerate((wq_hbm, wk_hbm, wv_hbm)):
        loads.append(pltpu.make_async_copy(w, wts.at[i], load_sem.at[i + 1]))
    for load in loads:
        load.start()

    @pl.loop(1, nrow)
    def _(i):
        pl.semaphore_signal(
            barrier, inc=1, device_id=(lax.rem(row + i, nrow), col), device_id_type=MESH
        )

    @pl.loop(1, ncol)
    def _(i):
        other = lax.rem(col + i, ncol)
        pl.semaphore_signal(barrier, inc=1, device_id=(row, other), device_id_type=MESH)
        pl.semaphore_signal(barrier, inc=1, device_id=(sib, other), device_id_type=MESH)

    lane8 = lax.broadcasted_iota(jnp.int32, (8, 128), 1)
    row8 = lax.broadcasted_iota(jnp.int32, (8, 128), 0)
    codes = jnp.zeros((8, 128), jnp.int32)
    for b in range(SLOTS_BLK):
        codes = jnp.where((lane8 == owner_ref[0, b]) & (row8 == 0), row * 8 + b + 1, codes)
    codes_tx[...] = codes
    codes_rx[row] = codes

    slot_ids = lax.broadcasted_iota(jnp.int32, (slots, map_ref.shape[1]), 0)
    hot = jnp.where(slot_ids == map_ref[...], 1.0, 0.0).astype(jnp.bfloat16)
    onehot[...] = hot
    count = jnp.dot(
        hot, jnp.ones((map_ref.shape[1], 128), jnp.bfloat16), preferred_element_type=jnp.float32
    )
    share = 1.0 / jnp.maximum(count, 1.0)

    def merge(which, dst, base):
        sums = jnp.dot(
            onehot[...],
            tok[:, pl.ds(pl.multiple_of(which * half, 128), half)],
            preferred_element_type=jnp.float32,
        )
        for i in range(half // 128):
            cols = slice(i * 128, (i + 1) * 128)
            part = (sums[:, cols] * share).astype(jnp.bfloat16)
            dst[pl.ds(base, SLOTS_BLK), :, cols] = part.reshape(SLOTS_BLK, BLK, 128)

    loads[0].wait()
    merge(1 - core, sib_tx, 0)

    pl.semaphore_wait(barrier, (nrow - 1) + 2 * (ncol - 1))

    def codes_copy(i, source):
        return pltpu.make_async_remote_copy(
            src_ref=codes_tx, dst_ref=codes_rx.at[source],
            send_sem=codes_ssem.at[i], recv_sem=codes_rsem.at[i],
            device_id=(lax.rem(row + i, nrow), col), device_id_type=MESH,
        )

    @pl.loop(1, nrow)
    def _(i):
        codes_copy(i, row).start()

    def pair_copy(i, src, dst):
        return pltpu.make_async_remote_copy(
            src_ref=src, dst_ref=dst, send_sem=pair_ssem.at[i], recv_sem=pair_rsem.at[i],
            device_id=(sib, col), device_id_type=MESH,
        )

    sib_copy = pair_copy(0, sib_tx, sib_rx)
    sib_copy.start()
    merge(core, local, core * SLOTS_BLK)

    @pl.loop(1, nrow)
    def _(i):
        codes_copy(i, lax.rem(row + nrow - i, nrow)).wait_recv()

    missed = plan_routes(codes_rx[...], tbl_v, nz, z, steps)
    tbl_copy = pltpu.make_async_copy(tbl_v, tbl_s, load_sem.at[4])
    tbl_copy.start()
    tbl_copy.wait()
    sib_copy.wait_recv()
    local[pl.ds((1 - core) * SLOTS_BLK, SLOTS_BLK)] = sib_rx[...]

    ahead = lax.rem(row + 2, nrow)
    behind = lax.rem(row + nrow - 2, nrow)

    def hop(t, d):
        return pltpu.make_async_remote_copy(
            src_ref=stage.at[d, t], dst_ref=recv.at[d, t],
            send_sem=hop_ssem.at[d, t], recv_sem=hop_rsem.at[d, t],
            device_id=(behind if d else ahead, col), device_id_type=MESH,
        )

    def take(t):
        for d in range(2):
            hop(t, d).wait_recv()
            local[16 + 2 * t + d] = recv[d, t]

    def put(t):
        for d in range(2):
            stage[d, t] = local[tbl_s[0, 2 * t + d]]
            hop(t, d).start()

    for t in range(DELAY):
        put(t)

    @pl.loop(DELAY, steps)
    def _(t):
        take(t - DELAY)
        put(t)

    for t in range(steps - DELAY, steps):
        take(t)

    for j in range(OWN):
        fin_tx[j] = local[tbl_s[2, OWN * (1 - core) + j]]
    fin_copy = pair_copy(1, fin_tx, fin_rx)
    fin_copy.start()
    for j in range(OWN):
        owned[core, j * BLK:(j + 1) * BLK] = local[tbl_s[2, OWN * core + j]]
    nb_tx[...] = jnp.where(row8 == 2, missed, 0)
    nb_tx[0:OWN, 0:nb_ref.shape[1]] = nb_ref[...]

    def nb_copy(i, source):
        return pltpu.make_async_remote_copy(
            src_ref=nb_tx, dst_ref=nb_rx.at[source],
            send_sem=nb_ssem.at[i], recv_sem=nb_rsem.at[i],
            device_id=(row, lax.rem(col + i, ncol)), device_id_type=MESH,
        )

    nb_rx[col] = nb_tx[...]

    @pl.loop(1, ncol)
    def _(i):
        nb_copy(i, col).start()

    for load in loads[1:]:
        load.wait()
    fin_copy.wait_recv()
    for j in range(OWN):
        owned[1 - core, j * BLK:(j + 1) * BLK] = fin_rx[j]
    left, right = owned[0], owned[1]

    def project(i):
        return (
            jnp.dot(left, wts[i, :half], preferred_element_type=jnp.float32)
            + jnp.dot(right, wts[i, half:], preferred_element_type=jnp.float32)
        ).astype(jnp.bfloat16)

    query, key, value = project(0), project(1), project(2)
    kv_rows = OWN * BLK
    for h in range(heads):
        cols = slice(h * HD, (h + 1) * HD)
        packed = jnp.concatenate([key[:, cols], value[:, cols]], axis=1)
        for j in range(OWN):
            q = query[j * BLK:(j + 1) * BLK, cols]
            msg_tx[OWN * h + j, 0:kv_rows] = packed
            msg_tx[OWN * h + j, kv_rows:kv_rows + BLK // 2] = jnp.concatenate(
                [q[: BLK // 2], q[BLK // 2:]], axis=1
            )

    def msg_copy(i, source):
        other = lax.rem(col + i, ncol)
        return pltpu.make_async_remote_copy(
            src_ref=msg_tx.at[other], dst_ref=msg_rx.at[source],
            send_sem=msg_ssem.at[i], recv_sem=msg_rsem.at[i],
            device_id=(row, other), device_id_type=MESH,
        )

    @pl.loop(1, ncol)
    def _(i):
        msg_copy(i, col).start()

    msg_rx[col] = msg_tx[col]

    def keep(source):
        pairs[pl.ds(OWN * source, OWN)] = msg_rx[source, 0:kv_rows].reshape(OWN, BLK, 128)

    keep(col)
    onehot_t[...] = onehot[...].T

    @pl.loop(1, ncol)
    def _(i):
        nb_copy(i, lax.rem(col + ncol - i, ncol)).wait_recv()

    nb_load = pltpu.make_async_copy(nb_rx, nb_s, load_sem.at[5])
    nb_load.start()
    flag_ref[...] = jnp.max(jnp.where(row8[None] == 2, nb_rx[...], 0), axis=0)
    nb_load.wait()

    @pl.loop(1, ncol)
    def _(i):
        source = lax.rem(col + ncol - i, ncol)
        msg_copy(i, source).wait_recv()
        keep(source)

    slot_q = lax.rem(col, OWN)
    to_core = col // half_col
    here = to_core == core
    low = lax.broadcasted_iota(jnp.int32, (BLK // 2, 128), 1) < HD
    factor = math.log2(math.e) / math.sqrt(HD)
    nb_count = nb_ref.shape[1]

    def att_copy(i):
        other = lax.rem(col + i, ncol)
        return pltpu.make_async_remote_copy(
            src_ref=att_tx.at[other],
            dst_ref=att_rx.at[core * half_col + lax.rem(col, half_col)],
            send_sem=att_ssem.at[i],
            recv_sem=att_rsem.at[core * half_col + lax.rem(col, half_col)],
            device_id=(2 * z + to_core, other), device_id_type=MESH,
        )

    @pl.loop(1, ncol + 1)
    def _(i):
        other = lax.rem(col + i, ncol)
        q2 = msg_rx[other, kv_rows:kv_rows + BLK // 2].astype(jnp.float32)
        q = jnp.concatenate(
            [jnp.where(low, q2, 0.0), jnp.where(low, pltpu.roll(q2, HD, 1), 0.0)], axis=0
        ).astype(jnp.bfloat16)
        tiles = []
        for n in range(nb_count):
            cand = nb_s[other, slot_q, n]
            tiles.append(pairs[cand])
        kv = jnp.concatenate(tiles, axis=0)
        score = lax.dot_general(
            q, kv, (((1,), (1,)), ((), ())), preferred_element_type=jnp.float32
        )
        top = jnp.max(score, axis=1, keepdims=True)
        prob = jnp.exp2((score - top) * factor)
        total = jnp.sum(prob, axis=1, keepdims=True)
        mix = jnp.dot(prob.astype(jnp.bfloat16), kv, preferred_element_type=jnp.float32) / total
        upper, lower = mix[: BLK // 2], mix[BLK // 2:]
        att_tx[other] = jnp.where(low, pltpu.roll(upper, HD, 1), lower).astype(jnp.bfloat16)

        @pl.when(jnp.logical_or(i < ncol, jnp.logical_not(here)))
        def _():
            att_copy(i).start()

    @pl.when(here)
    def _():
        att_rx[core * half_col + lax.rem(col, half_col)] = att_tx[col]

    def att_wait(i):
        pltpu.make_async_remote_copy(
            src_ref=att_tx.at[0], dst_ref=att_rx.at[i],
            send_sem=att_ssem.at[0], recv_sem=att_rsem.at[i],
            device_id=(row, col), device_id_type=MESH,
        ).wait_recv()

    @pl.loop(0, ncol)
    def _(i):
        own_turn = jnp.logical_and(here, i == core * half_col + lax.rem(col, half_col))

        @pl.when(jnp.logical_not(own_turn))
        def _():
            att_wait(i)

    for k in range(2):
        for j in range(OWN):
            for p in range(hh // 2):
                a = att_rx[k * half_col + (2 * p) * OWN + j].astype(jnp.float32)
                b = att_rx[k * half_col + (2 * p + 1) * OWN + j].astype(jnp.float32)
                cols = slice(p * 128, (p + 1) * 128)
                to = 2 * steps + k * OWN + j
                home[to, 0:BLK // 2, cols] = jnp.where(low, a, pltpu.roll(b, HD, 1)).astype(
                    jnp.bfloat16
                )
                home[to, BLK // 2:BLK, cols] = jnp.where(low, pltpu.roll(a, HD, 1), b).astype(
                    jnp.bfloat16
                )

    def ret(t, d):
        return pltpu.make_async_remote_copy(
            src_ref=ret_stage.at[d, t], dst_ref=ret_recv.at[d, t],
            send_sem=ret_ssem.at[d, t], recv_sem=ret_rsem.at[d, t],
            device_id=(ahead if d else behind, col), device_id_type=MESH,
        )

    def ret_take(t):
        for d in range(2):
            ret(t, d).wait_recv()
            home[2 * t + d] = ret_recv[d, t]

    def ret_put(t):
        for d in range(2):
            ret_stage[d, t] = home[tbl_s[1, 16 + 2 * t + d]]
            ret(t, d).start()

    for t in range(DELAY):
        ret_put(steps - 1 - t)

    @pl.loop(DELAY, steps)
    def _(s):
        ret_take(steps - 1 - s + DELAY)
        ret_put(steps - 1 - s)

    for t in reversed(range(DELAY)):
        ret_take(t)

    for b in range(SLOTS_BLK):
        ret_tx[b] = home[tbl_s[1, (1 - core) * SLOTS_BLK + b]]
    ret_copy = pair_copy(2, ret_tx, ret_rx)
    ret_copy.start()
    mine = jnp.concatenate([home[tbl_s[1, core * SLOTS_BLK + b]] for b in range(SLOTS_BLK)], axis=0)
    hot_t = onehot_t[...]
    out_ref[:, pl.ds(pl.multiple_of(core * hw, 128), hw)] = jnp.dot(
        hot_t, mine, preferred_element_type=jnp.float32
    ).astype(jnp.bfloat16)
    ret_copy.wait_recv()
    out_ref[:, pl.ds(pl.multiple_of((1 - core) * hw, 128), hw)] = jnp.dot(
        hot_t, ret_rx[...].reshape(slots, hw), preferred_element_type=jnp.float32
    ).astype(jnp.bfloat16)

    sib_copy.wait_send()
    fin_copy.wait_send()
    ret_copy.wait_send()

    @pl.loop(1, nrow)
    def _(i):
        codes_copy(i, row).wait_send()

    @pl.loop(1, ncol)
    def _(i):
        nb_copy(i, col).wait_send()
        msg_copy(i, col).wait_send()

    @pl.loop(1, ncol + 1)
    def _(i):
        @pl.when(jnp.logical_or(i < ncol, jnp.logical_not(here)))
        def _():
            att_copy(i).wait_send()

    @pl.loop(0, steps)
    def _(t):
        for d in range(2):
            hop(t, d).wait_send()
            ret(t, d).wait_send()


def routed(tokens, merge_map, block_owner, neighbours, w_query, w_key, w_value):
    nrow, ncol = lax.axis_size("row"), lax.axis_size("col")
    count, width = tokens.shape
    head_width = w_query.shape[1]
    heads = head_width // HD
    half, hw = width // 2, head_width // 2
    bf, i32 = jnp.bfloat16, jnp.int32
    places = 16 + 2 * STEPS
    hbm = pl.BlockSpec(memory_space=pl.ANY)
    vmem = pl.BlockSpec(memory_space=pltpu.VMEM)
    smem = pl.BlockSpec(memory_space=pltpu.SMEM)
    dma = pltpu.SemaphoreType.DMA
    msg_rows = OWN * BLK + BLK // 2
    slots = SLOTS_BLK * BLK
    scratch = [
        pltpu.VMEM((count, width), bf),
        pltpu.VMEM((3, width, head_width), bf),
        pltpu.VMEM((slots, count), bf),
        pltpu.VMEM((count, slots), bf),
        pltpu.VMEM((8, 128), i32),
        pltpu.VMEM((nrow, 8, 128), i32),
        pltpu.VMEM((8, 128), i32),
        pltpu.SMEM((8, 128), i32),
        pltpu.VMEM((places, BLK, half), bf),
        pltpu.VMEM((SLOTS_BLK, BLK, half), bf),
        pltpu.VMEM((SLOTS_BLK, BLK, half), bf),
        pltpu.VMEM((2, STEPS, BLK, half), bf),
        pltpu.VMEM((2, STEPS, BLK, half), bf),
        pltpu.VMEM((OWN, BLK, half), bf),
        pltpu.VMEM((OWN, BLK, half), bf),
        pltpu.VMEM((2, OWN * BLK, half), bf),
        pltpu.VMEM((ncol, msg_rows, 128), bf),
        pltpu.VMEM((ncol, msg_rows, 128), bf),
        pltpu.VMEM((OWN * ncol, BLK, 128), bf),
        pltpu.VMEM((8, 128), i32),
        pltpu.VMEM((ncol, 8, 128), i32),
        pltpu.SMEM((ncol, 8, 128), i32),
        pltpu.VMEM((ncol, BLK // 2, 128), bf),
        pltpu.VMEM((ncol, BLK // 2, 128), bf),
        pltpu.VMEM((2 * STEPS + 2 * OWN, BLK, hw), bf),
        pltpu.VMEM((2, STEPS, BLK, hw), bf),
        pltpu.VMEM((2, STEPS, BLK, hw), bf),
        pltpu.VMEM((SLOTS_BLK, BLK, hw), bf),
        pltpu.VMEM((SLOTS_BLK, BLK, hw), bf),
        dma((6,)),
        dma((nrow,)), dma((nrow,)),
        dma((3,)), dma((3,)),
        dma((2, STEPS)), dma((2, STEPS)),
        dma((ncol,)), dma((ncol,)),
        dma((ncol,)), dma((ncol,)),
        dma((ncol + 1,)), dma((ncol,)),
        dma((2, STEPS)), dma((2, STEPS)),
    ]
    return pl.pallas_call(
        functools.partial(kernel, (nrow, ncol, heads, width, STEPS)),
        out_shape=(
            jax.ShapeDtypeStruct((count, head_width), bf),
            jax.ShapeDtypeStruct((8, 128), i32),
        ),
        in_specs=[hbm, vmem, smem, vmem, hbm, hbm, hbm],
        out_specs=(vmem, vmem),
        scratch_shapes=scratch,
        compiler_params=pltpu.CompilerParams(
            collective_id=0, has_side_effects=True, vmem_limit_bytes=56 * 1024 * 1024
        ),
    )(tokens, merge_map.reshape(1, count), block_owner, neighbours, w_query, w_key, w_value)


def program(*args):
    out, missed = routed(*args)
    return lax.cond(missed[2, 0] > 0, lambda: on_device(*args), lambda: out)


def solution(mesh):
    in_specs = (
        P(("row", "col"), None),
        P(("row", "col")),
        P(("row", "col"), None),
        P(("row", "col"), None),
        P(),
        P(),
        P(),
    )
    out_specs = P(("row", "col"), None)
    return jax.shard_map(
        program, mesh=mesh, in_specs=in_specs, out_specs=out_specs, check_vma=False
    )
```

time: 443 us -> 144 us (0.33)
  waiting for transfers between devices: 346 us -> 0 us
  Pallas kernels: 0 us -> 127 us
  starting transfers between devices: 39.3 us -> 0 us
  matrix products: 19.4 us -> 0 us
  local copies, waits for them, and re-layouts: 16.3 us -> 2.01 us
  other arithmetic: 7.74 us -> 0 us
    all_to_all x3 -> x0, waiting for transfers between devices: 284 us -> none  [the longest x1 183 us: on_device(): lax.all_to_all(outgoing, 'row', split_axis=0, concat_axis=0, tiled=True)]
    pallas_call x0 -> x1, Pallas kernels: none -> 127 us  [routed(): pl.pallas_call(functools.partial(kernel, (nrow, ncol, heads, width, STEPS...]
    all_gather x1 -> x0, waiting for transfers between devices: 62.1 us -> none  [on_device(): token_piece = lax.all_gather(owned_tokens, 'col', axis=0, tiled=True)]
    all_to_all x3 -> x0, starting transfers between devices: 39.3 us -> none  [the longest x1 16.7 us: on_device(): lax.all_to_all(slot_tag, 'row', split_axis=0, concat_axis=0, tiled=True)]
    dot_general x10 -> x0, matrix products: 19.4 us -> none  [the longest x1 4.57 us: on_device(): jnp.dot(token_piece, w_key, preferred_element_type=jnp.float32)]
    unnamed x15 -> x13, local copies, waits for them, and re-layouts: 10.9 us -> 0.82 us
  transfers between devices with their start and end apart: 4 -> 0, of which waited for: 4 -> 0; matrix products, arithmetic and copies ran while one was open for 3% -> 0% of each run, Pallas kernels for 0% -> 0%
where the time goes in v1:
time: 144 us; the launch traced here: 143 us
  Pallas kernels  127 us (88%)
  between operations  14.1 us (10%)
  local copies, waits for them, and re-layouts  2.01 us (1%)
    pallas_call x1, Pallas kernels, routed(): pl.pallas_call(functools.partial(kernel, (nrow, ncol, heads, width, STEPS...  127 us

profile of v1, /device:TPU:1, one launch (start us, length us, event | category | flops | bytes accessed | tf_op | source)
XLA Modules:
  0.0 143.4 jit_solution(8129513249311839404)
XLA Ops:
  6.5 0.0 copy-start.1
  6.5 0.0 copy-start.4
  6.5 0.0 copy-start.6
  6.5 0.0 copy-start.5
  6.5 0.0 copy-start
  6.5 0.0 copy-start.2
  6.6 127.1 %shard_map.75 = (bf16[512,512]{1,0:T(8,128)(2,1)S(1)}, s32[8,128]{1,0:T(8,128)}) custom-call(bf16[512,1024]{1,0:T(8,128)(2,1)} %tokens_hbm.1, s32[1,512]{1,0:T(1,128)} %bitcast.54, s32[1,8]{1,0:T(1,128)} %owner_ref.1, s32[2,16]{1,0:T(2,128)} %nb_ref.1, bf16[1024,512]{1,0:T(8,128)(2,1)} %wq_hbm.1, bf16[1024,512]{1,0:T(8,128)(2,1)} %wk_hbm.1, ...), custom_call_target="tpu_custom_call" | custom-call | tf_op jit(solution)/shard_map/pallas_call | solution.py:575
  133.6 1.2 slice.3
  135.5 0.0 copy-done.1
  135.5 0.0 copy-done.4
  135.5 0.0 copy-done.6
  135.5 0.0 copy-done.5
  135.5 0.0 copy-done
  135.5 0.0 copy-done.2
  135.6 0.2 conditional.1
  135.8 0.8 copy.36
Async XLA Ops:
  6.5 129.0 %copy-start.1 = (bf16[512,1024]{1,0:T(8,128)(2,1)S(1)}, bf16[512,1024]{1,0:T(8,128)(2,1)}, u32[]{:S(2)}) copy-start(bf16[512,1024]{1,0:T(8,128)(2,1)} %tokens_hbm.1) | copy-start | bytes 3145732
  6.5 129.0 %copy-start.4 = (s32[512]{0:T(512)S(1)}, s32[512]{0:T(512)}, u32[]{:S(2)}) copy-start(s32[512]{0:T(512)} %param.10) | copy-start | bytes 6148
  6.5 129.0 %copy-start.6 = (s32[1,8]{1,0:T(1,128)S(1)}, s32[1,8]{1,0:T(1,128)}, u32[]{:S(2)}) copy-start(s32[1,8]{1,0:T(1,128)} %owner_ref.1) | copy-start | bytes 100
  6.5 129.0 %copy-start.5 = (s32[2,16]{1,0:T(2,128)S(1)}, s32[2,16]{1,0:T(2,128)}, u32[]{:S(2)}) copy-start(s32[2,16]{1,0:T(2,128)} %nb_ref.1) | copy-start | bytes 388
  6.5 129.0 %copy-start = (bf16[1024,512]{1,0:T(8,128)(2,1)S(1)}, bf16[1024,512]{1,0:T(8,128)(2,1)}, u32[]{:S(2)}) copy-start(bf16[1024,512]{1,0:T(8,128)(2,1)} %wq_hbm.1) | copy-start | bytes 3145732
  6.5 129.0 %copy-start.2 = (bf16[1024,512]{1,0:T(8,128)(2,1)S(1)}, bf16[1024,512]{1,0:T(8,128)(2,1)}, u32[]{:S(2)}) copy-start(bf16[1024,512]{1,0:T(8,128)(2,1)} %wk_hbm.1) | copy-start | bytes 3145732

commit v2 on v1

v2 whole, which is shorter than its diff:
```python
import functools
import math

import jax
import jax.numpy as jnp
from jax import lax
from jax.experimental import pallas as pl
from jax.experimental.pallas import tpu as pltpu
from jax.sharding import PartitionSpec as P

HD = 64
BLK = 64
OWN = 2
SLOTS_BLK = 8
PARTS = 2
PART = BLK // PARTS
MESH = pl.DeviceIdType.MESH
DIST = (1, 2, 1, 1, 2, 1, 1, 2, 1, 1, 1, 2, 2, 1, 1, 1)
NEED = (0, 0, 0, 0, 1, 2, 3, 5, 7, 7, 8, 9, 11, 12, 13, 14)
FIXED_LAG = 3


def plan_start(place, nz, rows):
    shape = (rows, 128)
    place = jnp.broadcast_to(place, shape)
    lane = lax.broadcasted_iota(jnp.int32, shape, 1)
    valid = place > 0
    place = jnp.where(valid, place - 1, 0)
    pos = place >> 4
    fwd = ((lane >> 2) - pos) & (nz - 1)
    half = nz // 2
    right = (fwd < half) | ((fwd == half) & ((lane & 1) == 0))
    rem = jnp.where(valid, jnp.where(right, fwd, nz - fwd), 0)
    return lane, pos, jnp.where(right, 0, 1), rem, place & 15


def plan_first(place, tbl_v, nz):
    lane, _, way, rem, loc = plan_start(place, nz, 8)
    row = lax.broadcasted_iota(jnp.int32, (8, 128), 0)
    send = jnp.zeros((8, 128), jnp.int32)
    left = jnp.where(way == row, rem, 0)
    for t in range(len(DIST)):
        if NEED[t] == 0:
            key = jnp.where(left >= DIST[t], left * 128 + lane + 1, 0)
            best = jnp.max(key, axis=1, keepdims=True)
            pick = (key == best) & (key > 0)
            own = jnp.sum(jnp.where(pick, loc, 0), axis=1, keepdims=True)
            send = jnp.where(lane == t, own, send)
            left = jnp.where(pick, 0, left)
    tbl_v[...] = send


def plan_routes(place, tbl_v, nz, z, slots, fixed):
    rows = max(2 * nz, 8)
    shape = (rows, 128)
    lane, pos, way, rem, loc = plan_start(place, nz, rows)
    row = lax.broadcasted_iota(jnp.int32, shape, 0)
    row_way = jnp.where(row >= nz, 1, 0)
    at = pos + nz * way
    sign = 1 - 2 * way
    ready = jnp.zeros(shape, jnp.int32)
    send = jnp.zeros(shape, jnp.int32)
    back = jnp.full(shape, -1, jnp.int32)
    for t, (dist, need) in enumerate(slots):
        go = (at == row) & (rem >= dist) & (ready <= need)
        if fixed:
            go = go & (rem == nz // 2 - t // 4) & ((lane & 3) == t % 4)
        key = jnp.where(go, rem * 128 + lane + 1, 0)
        best = jnp.max(key, axis=1, keepdims=True)
        pick = jnp.where(key == best, jnp.minimum(key, 1), 0)
        moved = jnp.broadcast_to(jnp.max(pick, axis=0, keepdims=True), shape) > 0
        own = jnp.broadcast_to(jnp.sum(pick * (loc + 1), axis=1, keepdims=True), shape)
        send = jnp.where(lane == t, own, send)
        back = jnp.where(lane == own - 1, 2 * t + row_way, back)
        at = jnp.where(moved, (at & nz) | ((at + dist * sign) & (nz - 1)), at)
        rem = jnp.where(moved, rem - dist, rem)
        ready = jnp.where(moved, t + 1, ready)
        loc = jnp.where(moved, 16 + 2 * t + way, loc)
    count = len(slots)

    def line(value):
        return jnp.broadcast_to(value, (8, 128))

    right = line(jnp.sum(jnp.where(row == z, send, 0), axis=0, keepdims=True))
    left = line(jnp.sum(jnp.where(row == z + nz, send, 0), axis=0, keepdims=True))
    here = (row == z) | (row == z + nz)
    home = line(jnp.max(jnp.where(here, back, -1), axis=0, keepdims=True))
    home = jnp.where(home < 0, 2 * count, home)
    lane8 = lane[:8]
    final = jnp.zeros((8, 128), jnp.int32)
    for i in range(2 * OWN):
        end = jnp.sum(jnp.where(lane == 2 * OWN * z + i, loc, 0), axis=1, keepdims=True)[:8]
        home = jnp.where(lane8 == end, 2 * count + i, home)
        final = jnp.where(lane8 == i, end, final)
    row8 = row[:8]
    table = jnp.where(row8 == 0, jnp.maximum(right - 1, 0), jnp.maximum(left - 1, 0))
    tbl_v[...] = jnp.where(row8 < 2, table, jnp.where(row8 == 2, home, final))
    return line(jnp.max(rem, axis=1, keepdims=True)[:8])


def in_turn(slots, parts, lag, put, take):
    count = len(slots)
    if lag:
        for t in range(lag):
            for h in range(parts):
                put(t, h)

        @pl.loop(lag, count)
        def _(t):
            for h in range(parts):
                take(t - lag, h)
                put(t, h)

        for t in range(count - lag, count):
            for h in range(parts):
                take(t, h)
        return
    done = 0
    for t, need in enumerate(slots):
        for h in range(parts):
            for u in range(done, need):
                take(u, h)
            put(t, h)
        done = max(done, need)
    for u in range(done, count):
        for h in range(parts):
            take(u, h)


def kernel(
    dims,
    tokens_hbm, map_ref, owner_ref, nb_ref, wq_hbm, wk_hbm, wv_hbm,
    out_ref, flag_ref,
    tok, wts, onehot, onehot_t,
    codes_tx, codes_rx, codes_sib, tbl_v, tbl_s, first_v, first_s,
    local_a, local_b, sib_tx, sib_rx, stage, recv, fin_tx, fin_rx, owned,
    msg_tx, msg_rx, pairs, nb_tx, nb_rx, nb_s, miss_tx, miss_rx, miss_s,
    att_tx, att_rx, home, ret_stage, ret_recv, ret_tx, ret_rx,
    load_sem, codes_ssem, codes_rsem, pair_ssem, pair_rsem, hop_ssem, hop_rsem,
    msg_ssem, msg_rsem, nb_ssem, nb_rsem, miss_ssem, miss_rsem, att_ssem, att_rsem,
    ret_ssem, ret_rsem,
):
    nrow, ncol, heads, width, slot_plan, fixed = dims
    nz = nrow // 2
    steps = len(slot_plan)
    local = (local_a, local_b)
    half = width // 2
    hh = heads // 2
    hw = hh * HD
    half_col = ncol // 2
    slots = SLOTS_BLK * BLK
    row = lax.axis_index("row")
    col = lax.axis_index("col")
    z = row // 2
    core = lax.rem(row, 2)
    sib = row + 1 - 2 * core
    barrier = pltpu.get_barrier_semaphore()

    loads = [pltpu.make_async_copy(tokens_hbm, tok, load_sem.at[0])]
    for i, w in enumerate((wq_hbm, wk_hbm, wv_hbm)):
        loads.append(pltpu.make_async_copy(w, wts.at[i], load_sem.at[i + 1]))
    for load in loads:
        load.start()

    @pl.loop(1, nrow)
    def _(i):
        pl.semaphore_signal(
            barrier, inc=1, device_id=(lax.rem(row + i, nrow), col), device_id_type=MESH
        )

    @pl.loop(1, ncol)
    def _(i):
        other = lax.rem(col + i, ncol)
        pl.semaphore_signal(barrier, inc=1, device_id=(row, other), device_id_type=MESH)
        pl.semaphore_signal(barrier, inc=1, device_id=(sib, other), device_id_type=MESH)

    lane8 = lax.broadcasted_iota(jnp.int32, (8, 128), 1)
    row8 = lax.broadcasted_iota(jnp.int32, (8, 128), 0)
    codes = jnp.zeros((8, 128), jnp.int32)
    for b in range(SLOTS_BLK):
        codes = jnp.where((lane8 == owner_ref[0, b]) & (row8 == 0), row * 8 + b + 1, codes)
    codes_tx[...] = codes
    codes_rx[row] = codes

    slot_ids = lax.broadcasted_iota(jnp.int32, (slots, map_ref.shape[1]), 0)
    hot = jnp.where(slot_ids == map_ref[...], 1.0, 0.0).astype(jnp.bfloat16)
    onehot[...] = hot
    count = jnp.dot(
        hot, jnp.ones((map_ref.shape[1], 128), jnp.bfloat16), preferred_element_type=jnp.float32
    )
    share = 1.0 / jnp.maximum(count, 1.0)

    def merge(which, store):
        sums = jnp.dot(
            onehot[...],
            tok[:, pl.ds(pl.multiple_of(which * half, 128), half)],
            preferred_element_type=jnp.float32,
        )
        for i in range(half // 128):
            cols = slice(i * 128, (i + 1) * 128)
            part = (sums[:, cols] * share).astype(jnp.bfloat16)
            store(part.reshape(SLOTS_BLK, BLK, 128), cols)

    loads[0].wait()

    def to_sib(part, cols):
        sib_tx[:, :, cols] = part

    merge(1 - core, to_sib)

    pl.semaphore_wait(barrier, (nrow - 1) + 2 * (ncol - 1))

    def codes_copy(i, source):
        return pltpu.make_async_remote_copy(
            src_ref=codes_tx, dst_ref=codes_rx.at[source],
            send_sem=codes_ssem.at[i], recv_sem=codes_rsem.at[i],
            device_id=(lax.rem(row + i, nrow), col), device_id_type=MESH,
        )

    def pair_copy(i, src, dst):
        return pltpu.make_async_remote_copy(
            src_ref=src, dst_ref=dst, send_sem=pair_ssem.at[i], recv_sem=pair_rsem.at[i],
            device_id=(sib, col), device_id_type=MESH,
        )

    code_copy = pair_copy(3, codes_tx, codes_sib)
    code_copy.start()
    sib_copy = pair_copy(0, sib_tx, sib_rx)
    sib_copy.start()

    @pl.loop(1, nrow)
    def _(i):
        codes_copy(i, row).start()

    def to_own(part, cols):
        for h in range(PARTS):
            local[h][pl.ds(core * SLOTS_BLK, SLOTS_BLK), :, cols] = part[
                :, h * PART:(h + 1) * PART
            ]

    merge(core, to_own)

    def away(t, d):
        far = 2 * (1 if fixed else slot_plan[t][0])
        return lax.rem(row + (nrow - far if d else far), nrow)

    def hop(t, d, h):
        return pltpu.make_async_remote_copy(
            src_ref=stage.at[h, d, t], dst_ref=recv.at[h, d, t],
            send_sem=hop_ssem.at[h, d, t], recv_sem=hop_rsem.at[h, d, t],
            device_id=(away(t, d), col), device_id_type=MESH,
        )

    def take(t, h):
        for d in range(2):
            hop(t, d, h).wait_recv()
            local[h][16 + 2 * t + d] = recv[h, d, t]

    def put(t, h, table=tbl_s):
        for d in range(2):
            stage[h, d, t] = local[h][table[d, t]]
            hop(t, d, h).start()

    def sib_arrived():
        sib_copy.wait_recv()
        for h in range(PARTS):
            local[h][pl.ds((1 - core) * SLOTS_BLK, SLOTS_BLK)] = sib_rx[
                :, h * PART:(h + 1) * PART
            ]

    early = 0 if fixed else sum(need == 0 for _, need in slot_plan)
    code_copy.wait_recv()
    if early:
        near = jnp.sum(codes_tx[...] + codes_sib[...], axis=0, keepdims=True)
        plan_first(near, first_v, nz)
        first_copy = pltpu.make_async_copy(first_v, first_s, load_sem.at[6])
        first_copy.start()
        sib_arrived()
        first_copy.wait()
        for t in range(early):
            for h in range(PARTS):
                put(t, h, first_s)

    nb_tx[...] = jnp.zeros((8, 128), jnp.int32)
    nb_tx[0:OWN, 0:nb_ref.shape[1]] = nb_ref[...]

    def plane_copy(i, source, src, dst, ssem, rsem):
        return pltpu.make_async_remote_copy(
            src_ref=src, dst_ref=dst.at[source], send_sem=ssem.at[i], recv_sem=rsem.at[i],
            device_id=(row, lax.rem(col + i, ncol)), device_id_type=MESH,
        )

    def nb_copy(i, source):
        return plane_copy(i, source, nb_tx, nb_rx, nb_ssem, nb_rsem)

    def miss_copy(i, source):
        return plane_copy(i, source, miss_tx, miss_rx, miss_ssem, miss_rsem)

    nb_rx[col] = nb_tx[...]

    @pl.loop(1, ncol)
    def _(i):
        nb_copy(i, col).start()

    @pl.loop(1, nrow)
    def _(i):
        codes_copy(i, lax.rem(row + nrow - i, nrow)).wait_recv()

    place = jnp.sum(jnp.sum(codes_rx[...], axis=0), axis=0, keepdims=True)
    miss_tx[...] = plan_routes(place, tbl_v, nz, z, slot_plan, fixed)
    tbl_copy = pltpu.make_async_copy(tbl_v, tbl_s, load_sem.at[4])
    tbl_copy.start()
    tbl_copy.wait()
    if not early:
        sib_arrived()
    needs = [need for _, need in slot_plan]

    def put_late(t, h):
        if fixed or t >= early:
            put(t, h)

    in_turn(needs, PARTS, FIXED_LAG if fixed else 0, put_late, take)

    for j in range(OWN):
        for h in range(PARTS):
            fin_tx[j, h * PART:(h + 1) * PART] = local[h][tbl_s[3, OWN * (1 - core) + j]]
    fin_copy = pair_copy(1, fin_tx, fin_rx)
    fin_copy.start()
    for j in range(OWN):
        for h in range(PARTS):
            base = j * BLK + h * PART
            owned[core, base:base + PART] = local[h][tbl_s[3, OWN * core + j]]
    for load in loads[1:]:
        load.wait()
    fin_copy.wait_recv()
    for j in range(OWN):
        owned[1 - core, j * BLK:(j + 1) * BLK] = fin_rx[j]
    left, right = owned[0], owned[1]

    def project(i):
        return (
            jnp.dot(left, wts[i, :half], preferred_element_type=jnp.float32)
            + jnp.dot(right, wts[i, half:], preferred_element_type=jnp.float32)
        ).astype(jnp.bfloat16)

    query, key, value = project(0), project(1), project(2)
    kv_rows = OWN * BLK
    for h in range(heads):
        cols = slice(h * HD, (h + 1) * HD)
        packed = jnp.concatenate([key[:, cols], value[:, cols]], axis=1)
        for j in range(OWN):
            q = query[j * BLK:(j + 1) * BLK, cols]
            msg_tx[OWN * h + j, 0:kv_rows] = packed
            msg_tx[OWN * h + j, kv_rows:kv_rows + BLK // 2] = jnp.concatenate(
                [q[: BLK // 2], q[BLK // 2:]], axis=1
            )

    def msg_copy(i, source):
        other = lax.rem(col + i, ncol)
        return pltpu.make_async_remote_copy(
            src_ref=msg_tx.at[other], dst_ref=msg_rx.at[source],
            send_sem=msg_ssem.at[i], recv_sem=msg_rsem.at[i],
            device_id=(row, other), device_id_type=MESH,
        )

    @pl.loop(1, ncol)
    def _(i):
        msg_copy(i, col).start()

    msg_rx[col] = msg_tx[col]

    def keep(source):
        pairs[pl.ds(OWN * source, OWN)] = msg_rx[source, 0:kv_rows].reshape(OWN, BLK, 128)

    keep(col)
    onehot_t[...] = onehot[...].T

    @pl.loop(1, ncol)
    def _(i):
        nb_copy(i, lax.rem(col + ncol - i, ncol)).wait_recv()

    nb_load = pltpu.make_async_copy(nb_rx, nb_s, load_sem.at[5])
    nb_load.start()
    nb_load.wait()

    @pl.loop(1, ncol)
    def _(i):
        source = lax.rem(col + ncol - i, ncol)
        msg_copy(i, source).wait_recv()
        keep(source)

    slot_q = lax.rem(col, OWN)
    to_core = col // half_col
    here = to_core == core
    low = lax.broadcasted_iota(jnp.int32, (BLK // 2, 128), 1) < HD
    factor = math.log2(math.e) / math.sqrt(HD)
    nb_count = nb_ref.shape[1]

    def att_copy(i):
        other = lax.rem(col + i, ncol)
        return pltpu.make_async_remote_copy(
            src_ref=att_tx.at[other],
            dst_ref=att_rx.at[core * half_col + lax.rem(col, half_col)],
            send_sem=att_ssem.at[i],
            recv_sem=att_rsem.at[core * half_col + lax.rem(col, half_col)],
            device_id=(2 * z + to_core, other), device_id_type=MESH,
        )

    @pl.loop(1, ncol + 1)
    def _(i):
        other = lax.rem(col + i, ncol)
        q2 = msg_rx[other, kv_rows:kv_rows + BLK // 2].astype(jnp.float32)
        q = jnp.concatenate(
            [jnp.where(low, q2, 0.0), jnp.where(low, pltpu.roll(q2, HD, 1), 0.0)], axis=0
        ).astype(jnp.bfloat16)
        tiles = []
        for n in range(nb_count):
            cand = nb_s[other, slot_q, n]
            tiles.append(pairs[cand])
        kv = jnp.concatenate(tiles, axis=0)
        score = lax.dot_general(
            q, kv, (((1,), (1,)), ((), ())), preferred_element_type=jnp.float32
        )
        top = jnp.max(score, axis=1, keepdims=True)
        prob = jnp.exp2((score - top) * factor)
        total = jnp.sum(prob, axis=1, keepdims=True)
        mix = jnp.dot(prob.astype(jnp.bfloat16), kv, preferred_element_type=jnp.float32) / total
        upper, lower = mix[: BLK // 2], mix[BLK // 2:]
        att_tx[other] = jnp.where(low, pltpu.roll(upper, HD, 1), lower).astype(jnp.bfloat16)

        @pl.when(jnp.logical_or(i < ncol, jnp.logical_not(here)))
        def _():
            att_copy(i).start()

    @pl.when(here)
    def _():
        att_rx[core * half_col + lax.rem(col, half_col)] = att_tx[col]

    def att_wait(i):
        pltpu.make_async_remote_copy(
            src_ref=att_tx.at[0], dst_ref=att_rx.at[i],
            send_sem=att_ssem.at[0], recv_sem=att_rsem.at[i],
            device_id=(row, col), device_id_type=MESH,
        ).wait_recv()

    @pl.loop(0, ncol)
    def _(i):
        own_turn = jnp.logical_and(here, i == core * half_col + lax.rem(col, half_col))

        @pl.when(jnp.logical_not(own_turn))
        def _():
            att_wait(i)

    for k in range(2):
        for j in range(OWN):
            for p in range(hh // 2):
                a = att_rx[k * half_col + (2 * p) * OWN + j].astype(jnp.float32)
                b = att_rx[k * half_col + (2 * p + 1) * OWN + j].astype(jnp.float32)
                cols = slice(p * 128, (p + 1) * 128)
                to = 2 * steps + k * OWN + j
                home[to, 0:BLK // 2, cols] = jnp.where(low, a, pltpu.roll(b, HD, 1)).astype(
                    jnp.bfloat16
                )
                home[to, BLK // 2:BLK, cols] = jnp.where(low, pltpu.roll(a, HD, 1), b).astype(
                    jnp.bfloat16
                )

    def ret(t, d):
        return pltpu.make_async_remote_copy(
            src_ref=ret_stage.at[d, t], dst_ref=ret_recv.at[d, t],
            send_sem=ret_ssem.at[d, t], recv_sem=ret_rsem.at[d, t],
            device_id=(away(t, 1 - d), col), device_id_type=MESH,
        )

    def ret_take(s, _):
        t = steps - 1 - s
        for d in range(2):
            ret(t, d).wait_recv()
            home[2 * t + d] = ret_recv[d, t]

    def ret_put(s, _):
        t = steps - 1 - s
        for d in range(2):
            ret_stage[d, t] = home[tbl_s[2, 16 + 2 * t + d]]
            ret(t, d).start()
        if not fixed and s == 1:
            tell()

    def tell():
        @pl.loop(1, ncol)
        def _(i):
            miss_copy(i, col).start()

    if fixed:
        tell()
    ret_needs = [
        steps - min([u for u in range(steps) if needs[u] > t], default=steps)
        for t in reversed(range(steps))
    ]
    in_turn(ret_needs, 1, FIXED_LAG if fixed else 0, ret_put, ret_take)

    for b in range(SLOTS_BLK):
        ret_tx[b] = home[tbl_s[2, (1 - core) * SLOTS_BLK + b]]
    ret_copy = pair_copy(2, ret_tx, ret_rx)
    ret_copy.start()
    mine = jnp.concatenate([home[tbl_s[2, core * SLOTS_BLK + b]] for b in range(SLOTS_BLK)], axis=0)
    hot_t = onehot_t[...]
    out_ref[:, pl.ds(pl.multiple_of(core * hw, 128), hw)] = jnp.dot(
        hot_t, mine, preferred_element_type=jnp.float32
    ).astype(jnp.bfloat16)
    miss_rx[col] = miss_tx[...]

    @pl.loop(1, ncol)
    def _(i):
        miss_copy(i, lax.rem(col + ncol - i, ncol)).wait_recv()

    first_v[...] = jnp.max(miss_rx[...], axis=0)
    miss_load = pltpu.make_async_copy(first_v, miss_s, load_sem.at[7])
    miss_load.start()
    miss_load.wait()
    flag_ref[0] = miss_s[0, 0]
    ret_copy.wait_recv()
    out_ref[:, pl.ds(pl.multiple_of((1 - core) * hw, 128), hw)] = jnp.dot(
        hot_t, ret_rx[...].reshape(slots, hw), preferred_element_type=jnp.float32
    ).astype(jnp.bfloat16)

    code_copy.wait_send()
    sib_copy.wait_send()
    fin_copy.wait_send()
    ret_copy.wait_send()

    @pl.loop(1, nrow)
    def _(i):
        codes_copy(i, row).wait_send()

    @pl.loop(1, ncol)
    def _(i):
        nb_copy(i, col).wait_send()
        miss_copy(i, col).wait_send()
        msg_copy(i, col).wait_send()

    @pl.loop(1, ncol + 1)
    def _(i):
        @pl.when(jnp.logical_or(i < ncol, jnp.logical_not(here)))
        def _():
            att_copy(i).wait_send()

    def sent(t):
        for d in range(2):
            for h in range(PARTS):
                hop(t, d, h).wait_send()
            ret(t, d).wait_send()

    if fixed:
        pl.loop(0, steps)(sent)
    else:
        for t in range(steps):
            sent(t)


def routed(fixed, tokens, merge_map, block_owner, neighbours, w_query, w_key, w_value):
    nrow, ncol = lax.axis_size("row"), lax.axis_size("col")
    count, width = tokens.shape
    head_width = w_query.shape[1]
    heads = head_width // HD
    half, hw = width // 2, head_width // 2
    bf, i32 = jnp.bfloat16, jnp.int32
    if fixed:
        slot_plan = tuple((1, max(0, t - FIXED_LAG + 1)) for t in range(nrow))
    else:
        slot_plan = tuple(zip(DIST, NEED))
    steps = len(slot_plan)
    places = 16 + 2 * steps
    hbm = pl.BlockSpec(memory_space=pl.ANY)
    vmem = pl.BlockSpec(memory_space=pltpu.VMEM)
    smem = pl.BlockSpec(memory_space=pltpu.SMEM)
    dma = pltpu.SemaphoreType.DMA
    msg_rows = OWN * BLK + BLK // 2
    slots = SLOTS_BLK * BLK
    scratch = [
        pltpu.VMEM((count, width), bf),
        pltpu.VMEM((3, width, head_width), bf),
        pltpu.VMEM((slots, count), bf),
        pltpu.VMEM((count, slots), bf),
        pltpu.VMEM((8, 128), i32),
        pltpu.VMEM((nrow, 8, 128), i32),
        pltpu.VMEM((8, 128), i32),
        pltpu.VMEM((8, 128), i32),
        pltpu.SMEM((8, 128), i32),
        pltpu.VMEM((8, 128), i32),
        pltpu.SMEM((8, 128), i32),
        pltpu.VMEM((places, PART, half), bf),
        pltpu.VMEM((places, PART, half), bf),
        pltpu.VMEM((SLOTS_BLK, BLK, half), bf),
        pltpu.VMEM((SLOTS_BLK, BLK, half), bf),
        pltpu.VMEM((PARTS, 2, steps, PART, half), bf),
        pltpu.VMEM((PARTS, 2, steps, PART, half), bf),
        pltpu.VMEM((OWN, BLK, half), bf),
        pltpu.VMEM((OWN, BLK, half), bf),
        pltpu.VMEM((2, OWN * BLK, half), bf),
        pltpu.VMEM((ncol, msg_rows, 128), bf),
        pltpu.VMEM((ncol, msg_rows, 128), bf),
        pltpu.VMEM((OWN * ncol, BLK, 128), bf),
        pltpu.VMEM((8, 128), i32),
        pltpu.VMEM((ncol, 8, 128), i32),
        pltpu.SMEM((ncol, 8, 128), i32),
        pltpu.VMEM((8, 128), i32),
        pltpu.VMEM((ncol, 8, 128), i32),
        pltpu.SMEM((8, 128), i32),
        pltpu.VMEM((ncol, BLK // 2, 128), bf),
        pltpu.VMEM((ncol, BLK // 2, 128), bf),
        pltpu.VMEM((2 * steps + 2 * OWN, BLK, hw), bf),
        pltpu.VMEM((2, steps, BLK, hw), bf),
        pltpu.VMEM((2, steps, BLK, hw), bf),
        pltpu.VMEM((SLOTS_BLK, BLK, hw), bf),
        pltpu.VMEM((SLOTS_BLK, BLK, hw), bf),
        dma((8,)),
        dma((nrow,)), dma((nrow,)),
        dma((4,)), dma((4,)),
        dma((PARTS, 2, steps)), dma((PARTS, 2, steps)),
        dma((ncol,)), dma((ncol,)),
        dma((ncol,)), dma((ncol,)),
        dma((ncol,)), dma((ncol,)),
        dma((ncol + 1,)), dma((ncol,)),
        dma((2, steps)), dma((2, steps)),
    ]
    return pl.pallas_call(
        functools.partial(kernel, (nrow, ncol, heads, width, slot_plan, fixed)),
        out_shape=(
            jax.ShapeDtypeStruct((count, head_width), bf),
            jax.ShapeDtypeStruct((1,), i32),
        ),
        in_specs=[hbm, vmem, smem, vmem, hbm, hbm, hbm],
        out_specs=(vmem, smem),
        scratch_shapes=scratch,
        compiler_params=pltpu.CompilerParams(
            collective_id=int(fixed), has_side_effects=True, vmem_limit_bytes=56 * 1024 * 1024
        ),
    )(tokens, merge_map.reshape(1, count), block_owner, neighbours, w_query, w_key, w_value)


def program(*args):
    out, missed = routed(False, *args)
    return lax.cond(missed[0] > 0, lambda: routed(True, *args)[0], lambda: out)


def solution(mesh):
    in_specs = (
        P(("row", "col"), None),
        P(("row", "col")),
        P(("row", "col"), None),
        P(("row", "col"), None),
        P(),
        P(),
        P(),
    )
    out_specs = P(("row", "col"), None)
    return jax.shard_map(
        program, mesh=mesh, in_specs=in_specs, out_specs=out_specs, check_vma=False
    )
```

time: 144 us -> 115 us (0.80)
  Pallas kernels: 127 us -> 113 us
  between operations: 14.1 us -> 0.7 us
    pallas_call x1, Pallas kernels: 127 us -> 113 us  [routed(): pl.pallas_call(functools.partial(kernel, (nrow, ncol, heads, width, slot_...]
where the time goes in v2:
time: 115 us
  Pallas kernels  113 us (98%)
  local copies, waits for them, and re-layouts  1.5 us (1%)
    pallas_call x1, Pallas kernels, routed(): pl.pallas_call(functools.partial(kernel, (nrow, ncol, heads, width, slot_...  113 us

profile of v2, /device:TPU:1, one launch (start us, length us, event | category | flops | bytes accessed | tf_op | source)
XLA Modules:
  0.0 115.4 jit_solution(8682102539120660069)
XLA Ops:
  0.0 0.0 copy-start.4
  0.0 0.0 copy-start.5
  0.0 0.0 copy-start.6
  0.0 0.7 copy-done.4
  0.7 0.0 copy-done.5
  0.7 0.0 copy-done.6
  0.7 0.0 copy-start
  0.7 0.0 copy-start.1
  0.7 0.0 copy-start.2
  0.7 0.0 copy-start.3
  0.7 113.2 %shard_map.75 = (bf16[512,512]{1,0:T(8,128)(2,1)S(1)}, s32[1]{0:T(128)}) custom-call(bf16[512,1024]{1,0:T(8,128)(2,1)} %tokens_hbm.1, s32[1,512]{1,0:T(1,128)S(1)} %bitcast.3, s32[1,8]{1,0:T(1,128)S(1)} %copy-done.6, s32[2,16]{1,0:T(2,128)S(1)} %copy-done.5, bf16[1024,512]{1,0:T(8,128)(2,1)} %wq_hbm.1, bf16[1024,512]{1,0:T(8,128)(2,1)} %wk_hbm.1, ...), custom_call_target="tpu_custom_call" | custom-call | tf_op jit(solution)/shard_map/pallas_call | solution.py:627
  114.5 0.0 copy-done
  114.5 0.0 copy-done.1
  114.5 0.0 copy-done.2
  114.6 0.0 copy-done.3
  114.6 0.8 copy.13
  (1 shorter events, 0.0 us)
Async XLA Ops:
  0.0 0.7 copy-start.4
  0.0 0.7 copy-start.5
  0.0 0.7 copy-start.6
  0.7 113.8 %copy-start = (bf16[512,1024]{1,0:T(8,128)(2,1)S(1)}, bf16[512,1024]{1,0:T(8,128)(2,1)}, u32[]{:S(2)}) copy-start(bf16[512,1024]{1,0:T(8,128)(2,1)} %tokens_hbm.1) | copy-start | bytes 3145732
  0.7 113.8 %copy-start.1 = (bf16[1024,512]{1,0:T(8,128)(2,1)S(1)}, bf16[1024,512]{1,0:T(8,128)(2,1)}, u32[]{:S(2)}) copy-start(bf16[1024,512]{1,0:T(8,128)(2,1)} %wq_hbm.1) | copy-start | bytes 3145732
  0.7 113.8 %copy-start.2 = (bf16[1024,512]{1,0:T(8,128)(2,1)S(1)}, bf16[1024,512]{1,0:T(8,128)(2,1)}, u32[]{:S(2)}) copy-start(bf16[1024,512]{1,0:T(8,128)(2,1)} %wk_hbm.1) | copy-start | bytes 3145732
  0.7 113.8 %copy-start.3 = (bf16[1024,512]{1,0:T(8,128)(2,1)S(1)}, bf16[1024,512]{1,0:T(8,128)(2,1)}, u32[]{:S(2)}) copy-start(bf16[1024,512]{1,0:T(8,128)(2,1)} %wv_hbm.1) | copy-start | bytes 3145732

commit v3 on v2

--- a/solution.py
+++ b/solution.py
@@ -14,6 +14,7 @@
 SLOTS_BLK = 8
 PARTS = 2
 PART = BLK // PARTS
+TOGETHER = 4
 MESH = pl.DeviceIdType.MESH
 DIST = (1, 2, 1, 1, 2, 1, 1, 2, 1, 1, 1, 2, 2, 1, 1, 1)
 NEED = (0, 0, 0, 0, 1, 2, 3, 5, 7, 7, 8, 9, 11, 12, 13, 14)
@@ -129,21 +130,22 @@
 
 def kernel(
     dims,
-    tokens_hbm, map_ref, owner_ref, nb_ref, wq_hbm, wk_hbm, wv_hbm,
+    tokens_hbm, map_hbm, owner_hbm, nb_hbm, wq_hbm, wk_hbm, wv_hbm,
     out_ref, flag_ref,
-    tok, wts, onehot, onehot_t,
+    tok, wts, map_ref, owner_ref, nb_ref, onehot, onehot_t,
     codes_tx, codes_rx, codes_sib, tbl_v, tbl_s, first_v, first_s,
-    local_a, local_b, sib_tx, sib_rx, stage, recv, fin_tx, fin_rx, owned,
+    sib_tx, sib_rx, stage, recv, fin_tx, fin_rx, owned,
     msg_tx, msg_rx, pairs, nb_tx, nb_rx, nb_s, miss_tx, miss_rx, miss_s,
-    att_tx, att_rx, home, ret_stage, ret_recv, ret_tx, ret_rx,
+    att_tx, att_rx, ret_stage, ret_recv, ret_tx, ret_rx,
     load_sem, codes_ssem, codes_rsem, pair_ssem, pair_rsem, hop_ssem, hop_rsem,
     msg_ssem, msg_rsem, nb_ssem, nb_rsem, miss_ssem, miss_rsem, att_ssem, att_rsem,
-    ret_ssem, ret_rsem,
+    ret_ssem, ret_rsem, *kept,
 ):
     nrow, ncol, heads, width, slot_plan, fixed = dims
     nz = nrow // 2
     steps = len(slot_plan)
-    local = (local_a, local_b)
+    local, home = kept[:PARTS], kept[PARTS:]
+    side = math.isqrt(ncol)
     half = width // 2
     hh = heads // 2
     hw = hh * HD
@@ -156,23 +158,43 @@
     sib = row + 1 - 2 * core
     barrier = pltpu.get_barrier_semaphore()
 
+    small = [
+        pltpu.make_async_copy(src, dst, load_sem.at[8 + i])
+        for i, (src, dst) in enumerate(
+            ((owner_hbm, owner_ref), (map_hbm, map_ref), (nb_hbm, nb_ref))
+        )
+    ]
+    for copy in small:
+        copy.start()
     loads = [pltpu.make_async_copy(tokens_hbm, tok, load_sem.at[0])]
     for i, w in enumerate((wq_hbm, wk_hbm, wv_hbm)):
         loads.append(pltpu.make_async_copy(w, wts.at[i], load_sem.at[i + 1]))
     for load in loads:
         load.start()
 
-    @pl.loop(1, nrow)
+    def ring(i):
+        return nrow // 2 + ((i + 1) // 2) * (1 - 2 * lax.rem(i, 2))
+
+    def plane(i, sign=1):
+        dx, dy = (0x36 >> (2 * (i // side))) & 3, (0x36 >> (2 * lax.rem(i, side))) & 3
+        x = lax.rem(col // side + side + sign * dx, side)
+        y = lax.rem(lax.rem(col, side) + side + sign * dy, side)
+        return x * side + y
+
+    @pl.loop(0, nrow - 1)
     def _(i):
         pl.semaphore_signal(
-            barrier, inc=1, device_id=(lax.rem(row + i, nrow), col), device_id_type=MESH
-        )
-
-    @pl.loop(1, ncol)
-    def _(i):
-        other = lax.rem(col + i, ncol)
+            barrier, inc=1, device_id=(lax.rem(row + ring(i), nrow), col), device_id_type=MESH
+        )
+
+    @pl.loop(0, ncol - 1)
+    def _(i):
+        other = plane(i)
         pl.semaphore_signal(barrier, inc=1, device_id=(row, other), device_id_type=MESH)
         pl.semaphore_signal(barrier, inc=1, device_id=(sib, other), device_id_type=MESH)
+
+    for copy in small:
+        copy.wait()
 
     lane8 = lax.broadcasted_iota(jnp.int32, (8, 128), 1)
     row8 = lax.broadcasted_iota(jnp.int32, (8, 128), 0)
@@ -208,30 +230,6 @@
 
     merge(1 - core, to_sib)
 
-    pl.semaphore_wait(barrier, (nrow - 1) + 2 * (ncol - 1))
-
-    def codes_copy(i, source):
-        return pltpu.make_async_remote_copy(
-            src_ref=codes_tx, dst_ref=codes_rx.at[source],
-            send_sem=codes_ssem.at[i], recv_sem=codes_rsem.at[i],
-            device_id=(lax.rem(row + i, nrow), col), device_id_type=MESH,
-        )
-
-    def pair_copy(i, src, dst):
-        return pltpu.make_async_remote_copy(
-            src_ref=src, dst_ref=dst, send_sem=pair_ssem.at[i], recv_sem=pair_rsem.at[i],
-            device_id=(sib, col), device_id_type=MESH,
-        )
-
-    code_copy = pair_copy(3, codes_tx, codes_sib)
-    code_copy.start()
-    sib_copy = pair_copy(0, sib_tx, sib_rx)
-    sib_copy.start()
-
-    @pl.loop(1, nrow)
-    def _(i):
-        codes_copy(i, row).start()
-
     def to_own(part, cols):
         for h in range(PARTS):
             local[h][pl.ds(core * SLOTS_BLK, SLOTS_BLK), :, cols] = part[
@@ -239,6 +237,30 @@
             ]
 
     merge(core, to_own)
+    onehot_t[...] = onehot[...].T
+    pl.semaphore_wait(barrier, (nrow - 1) + 2 * (ncol - 1))
+
+    def codes_copy(i, source):
+        return pltpu.make_async_remote_copy(
+            src_ref=codes_tx, dst_ref=codes_rx.at[source],
+            send_sem=codes_ssem.at[i], recv_sem=codes_rsem.at[i],
+            device_id=(lax.rem(row + ring(i), nrow), col), device_id_type=MESH,
+        )
+
+    def pair_copy(i, src, dst):
+        return pltpu.make_async_remote_copy(
+            src_ref=src, dst_ref=dst, send_sem=pair_ssem.at[i], recv_sem=pair_rsem.at[i],
+            device_id=(sib, col), device_id_type=MESH,
+        )
+
+    code_copy = pair_copy(3, codes_tx, codes_sib)
+    code_copy.start()
+    sib_copy = pair_copy(0, sib_tx, sib_rx)
+    sib_copy.start()
+
+    @pl.loop(0, nrow - 1)
+    def _(i):
+        codes_copy(i, row).start()
 
     def away(t, d):
         far = 2 * (1 if fixed else slot_plan[t][0])
@@ -287,7 +309,7 @@
     def plane_copy(i, source, src, dst, ssem, rsem):
         return pltpu.make_async_remote_copy(
             src_ref=src, dst_ref=dst.at[source], send_sem=ssem.at[i], recv_sem=rsem.at[i],
-            device_id=(row, lax.rem(col + i, ncol)), device_id_type=MESH,
+            device_id=(row, plane(i)), device_id_type=MESH,
         )
 
     def nb_copy(i, source):
@@ -298,13 +320,13 @@
 
     nb_rx[col] = nb_tx[...]
 
-    @pl.loop(1, ncol)
+    @pl.loop(0, ncol - 1)
     def _(i):
         nb_copy(i, col).start()
 
-    @pl.loop(1, nrow)
-    def _(i):
-        codes_copy(i, lax.rem(row + nrow - i, nrow)).wait_recv()
+    @pl.loop(0, nrow - 1)
+    def _(i):
+        codes_copy(i, lax.rem(row + nrow - ring(i), nrow)).wait_recv()
 
     place = jnp.sum(jnp.sum(codes_rx[...], axis=0), axis=0, keepdims=True)
     miss_tx[...] = plan_routes(place, tbl_v, nz, z, slot_plan, fixed)
@@ -332,61 +354,73 @@
             owned[core, base:base + PART] = local[h][tbl_s[3, OWN * core + j]]
     for load in loads[1:]:
         load.wait()
+
+    kv_rows = OWN * BLK
+
+    def msg_copy(other, source):
+        return pltpu.make_async_remote_copy(
+            src_ref=msg_tx.at[other], dst_ref=msg_rx.at[source],
+            send_sem=msg_ssem.at[other], recv_sem=msg_rsem.at[source],
+            device_id=(row, other), device_id_type=MESH,
+        )
+
+    def keep(source):
+        pairs[pl.ds(OWN * source, OWN)] = msg_rx[source, 0:kv_rows].reshape(OWN, BLK, 128)
+
+    def product(which, i, group):
+        return jnp.dot(
+            owned[which],
+            wts[
+                i,
+                pl.ds(pl.multiple_of(which * half, 128), half),
+                pl.ds(pl.multiple_of(group * hw, 128), hw),
+            ],
+            preferred_element_type=jnp.float32,
+        )
+
+    groups = [lax.rem(col + g, 2) for g in range(2)]
+    begun = [[product(core, i, group) for i in range(3)] for group in groups]
     fin_copy.wait_recv()
     for j in range(OWN):
         owned[1 - core, j * BLK:(j + 1) * BLK] = fin_rx[j]
-    left, right = owned[0], owned[1]
-
-    def project(i):
-        return (
-            jnp.dot(left, wts[i, :half], preferred_element_type=jnp.float32)
-            + jnp.dot(right, wts[i, half:], preferred_element_type=jnp.float32)
-        ).astype(jnp.bfloat16)
-
-    query, key, value = project(0), project(1), project(2)
-    kv_rows = OWN * BLK
-    for h in range(heads):
-        cols = slice(h * HD, (h + 1) * HD)
-        packed = jnp.concatenate([key[:, cols], value[:, cols]], axis=1)
-        for j in range(OWN):
-            q = query[j * BLK:(j + 1) * BLK, cols]
-            msg_tx[OWN * h + j, 0:kv_rows] = packed
-            msg_tx[OWN * h + j, kv_rows:kv_rows + BLK // 2] = jnp.concatenate(
-                [q[: BLK // 2], q[BLK // 2:]], axis=1
-            )
-
-    def msg_copy(i, source):
-        other = lax.rem(col + i, ncol)
-        return pltpu.make_async_remote_copy(
-            src_ref=msg_tx.at[other], dst_ref=msg_rx.at[source],
-            send_sem=msg_ssem.at[i], recv_sem=msg_rsem.at[i],
-            device_id=(row, other), device_id_type=MESH,
-        )
-
-    @pl.loop(1, ncol)
-    def _(i):
-        msg_copy(i, col).start()
+    for group, sums in zip(groups, begun):
+        query, key, value = (
+            (sums[i] + product(1 - core, i, group)).astype(jnp.bfloat16) for i in range(3)
+        )
+        for h in range(hh):
+            cols = slice(h * HD, (h + 1) * HD)
+            packed = jnp.concatenate([key[:, cols], value[:, cols]], axis=1)
+            for j in range(OWN):
+                q = query[j * BLK:(j + 1) * BLK, cols]
+                to = half_col * group + OWN * h + j
+                msg_tx[to, 0:kv_rows] = packed
+                msg_tx[to, kv_rows:kv_rows + BLK // 2] = jnp.concatenate(
+                    [q[: BLK // 2], q[BLK // 2:]], axis=1
+                )
+
+        @pl.loop(0, half_col)
+        def _(i):
+            other = half_col * group + lax.rem(col + half_col // 2 + i, half_col)
+
+            @pl.when(other != col)
+            def _():
+                msg_copy(other, col).start()
 
     msg_rx[col] = msg_tx[col]
-
-    def keep(source):
-        pairs[pl.ds(OWN * source, OWN)] = msg_rx[source, 0:kv_rows].reshape(OWN, BLK, 128)
-
     keep(col)
-    onehot_t[...] = onehot[...].T
-
-    @pl.loop(1, ncol)
-    def _(i):
-        nb_copy(i, lax.rem(col + ncol - i, ncol)).wait_recv()
+
+    @pl.loop(0, ncol - 1)
+    def _(i):
+        nb_copy(i, plane(i, -1)).wait_recv()
 
     nb_load = pltpu.make_async_copy(nb_rx, nb_s, load_sem.at[5])
     nb_load.start()
     nb_load.wait()
 
-    @pl.loop(1, ncol)
-    def _(i):
-        source = lax.rem(col + ncol - i, ncol)
-        msg_copy(i, source).wait_recv()
+    @pl.loop(0, ncol - 1)
+    def _(i):
+        source = lax.rem(col + 1 + i, ncol)
+        msg_copy(source, source).wait_recv()
         keep(source)
 
     slot_q = lax.rem(col, OWN)
@@ -397,7 +431,7 @@
     nb_count = nb_ref.shape[1]
 
     def att_copy(i):
-        other = lax.rem(col + i, ncol)
+        other = plane(i)
         return pltpu.make_async_remote_copy(
             src_ref=att_tx.at[other],
             dst_ref=att_rx.at[core * half_col + lax.rem(col, half_col)],
@@ -406,18 +440,12 @@
             device_id=(2 * z + to_core, other), device_id_type=MESH,
         )
 
-    @pl.loop(1, ncol + 1)
-    def _(i):
-        other = lax.rem(col + i, ncol)
+    def attend(other):
         q2 = msg_rx[other, kv_rows:kv_rows + BLK // 2].astype(jnp.float32)
         q = jnp.concatenate(
             [jnp.where(low, q2, 0.0), jnp.where(low, pltpu.roll(q2, HD, 1), 0.0)], axis=0
         ).astype(jnp.bfloat16)
-        tiles = []
-        for n in range(nb_count):
-            cand = nb_s[other, slot_q, n]
-            tiles.append(pairs[cand])
-        kv = jnp.concatenate(tiles, axis=0)
+        kv = jnp.concatenate([pairs[nb_s[other, slot_q, n]] for n in range(nb_count)], axis=0)
         score = lax.dot_general(
             q, kv, (((1,), (1,)), ((), ())), preferred_element_type=jnp.float32
         )
@@ -426,11 +454,19 @@
         total = jnp.sum(prob, axis=1, keepdims=True)
         mix = jnp.dot(prob.astype(jnp.bfloat16), kv, preferred_element_type=jnp.float32) / total
         upper, lower = mix[: BLK // 2], mix[BLK // 2:]
-        att_tx[other] = jnp.where(low, pltpu.roll(upper, HD, 1), lower).astype(jnp.bfloat16)
-
-        @pl.when(jnp.logical_or(i < ncol, jnp.logical_not(here)))
-        def _():
-            att_copy(i).start()
+        return jnp.where(low, pltpu.roll(upper, HD, 1), lower).astype(jnp.bfloat16)
+
+    @pl.loop(0, ncol, step=TOGETHER)
+    def _(first):
+        done = [attend(plane(first + n)) for n in range(TOGETHER)]
+        for n in range(TOGETHER):
+            att_tx[plane(first + n)] = done[n]
+        for n in range(TOGETHER):
+            i = first + n
+
+            @pl.when(jnp.logical_or(i < ncol - 1, jnp.logical_not(here)))
+            def _(i=i):
+                att_copy(i).start()
 
     @pl.when(here)
     def _():
@@ -458,36 +494,32 @@
                 b = att_rx[k * half_col + (2 * p + 1) * OWN + j].astype(jnp.float32)
                 cols = slice(p * 128, (p + 1) * 128)
                 to = 2 * steps + k * OWN + j
-                home[to, 0:BLK // 2, cols] = jnp.where(low, a, pltpu.roll(b, HD, 1)).astype(
-                    jnp.bfloat16
-                )
-                home[to, BLK // 2:BLK, cols] = jnp.where(low, pltpu.roll(a, HD, 1), b).astype(
-                    jnp.bfloat16
-                )
-
-    def ret(t, d):
+                home[0][to, :, cols] = jnp.where(low, a, pltpu.roll(b, HD, 1)).astype(jnp.bfloat16)
+                home[1][to, :, cols] = jnp.where(low, pltpu.roll(a, HD, 1), b).astype(jnp.bfloat16)
+
+    def ret(t, d, h):
         return pltpu.make_async_remote_copy(
-            src_ref=ret_stage.at[d, t], dst_ref=ret_recv.at[d, t],
-            send_sem=ret_ssem.at[d, t], recv_sem=ret_rsem.at[d, t],
+            src_ref=ret_stage.at[h, d, t], dst_ref=ret_recv.at[h, d, t],
+            send_sem=ret_ssem.at[h, d, t], recv_sem=ret_rsem.at[h, d, t],
             device_id=(away(t, 1 - d), col), device_id_type=MESH,
         )
 
-    def ret_take(s, _):
+    def ret_take(s, h):
         t = steps - 1 - s
         for d in range(2):
-            ret(t, d).wait_recv()
-            home[2 * t + d] = ret_recv[d, t]
-
-    def ret_put(s, _):
+            ret(t, d, h).wait_recv()
+            home[h][2 * t + d] = ret_recv[h, d, t]
+
+    def ret_put(s, h):
         t = steps - 1 - s
         for d in range(2):
-            ret_stage[d, t] = home[tbl_s[2, 16 + 2 * t + d]]
-            ret(t, d).start()
-        if not fixed and s == 1:
+            ret_stage[h, d, t] = home[h][tbl_s[2, 16 + 2 * t + d]]
+            ret(t, d, h).start()
+        if not fixed and s == 1 and h == 0:
             tell()
 
     def tell():
-        @pl.loop(1, ncol)
+        @pl.loop(0, ncol - 1)
         def _(i):
             miss_copy(i, col).start()
 
@@ -497,22 +529,26 @@
         steps - min([u for u in range(steps) if needs[u] > t], default=steps)
         for t in reversed(range(steps))
     ]
-    in_turn(ret_needs, 1, FIXED_LAG if fixed else 0, ret_put, ret_take)
+    in_turn(ret_needs, 2, FIXED_LAG if fixed else 0, ret_put, ret_take)
 
     for b in range(SLOTS_BLK):
-        ret_tx[b] = home[tbl_s[2, (1 - core) * SLOTS_BLK + b]]
+        at = tbl_s[2, (1 - core) * SLOTS_BLK + b]
+        for h in range(2):
+            ret_tx[b, h * (BLK // 2):(h + 1) * (BLK // 2)] = home[h][at]
     ret_copy = pair_copy(2, ret_tx, ret_rx)
     ret_copy.start()
-    mine = jnp.concatenate([home[tbl_s[2, core * SLOTS_BLK + b]] for b in range(SLOTS_BLK)], axis=0)
+    mine = jnp.concatenate(
+        [home[h][tbl_s[2, core * SLOTS_BLK + b]] for b in range(SLOTS_BLK) for h in range(2)], axis=0
+    )
     hot_t = onehot_t[...]
     out_ref[:, pl.ds(pl.multiple_of(core * hw, 128), hw)] = jnp.dot(
         hot_t, mine, preferred_element_type=jnp.float32
     ).astype(jnp.bfloat16)
     miss_rx[col] = miss_tx[...]
 
-    @pl.loop(1, ncol)
-    def _(i):
-        miss_copy(i, lax.rem(col + ncol - i, ncol)).wait_recv()
+    @pl.loop(0, ncol - 1)
+    def _(i):
+        miss_copy(i, plane(i, -1)).wait_recv()
 
     first_v[...] = jnp.max(miss_rx[...], axis=0)
     miss_load = pltpu.make_async_copy(first_v, miss_s, load_sem.at[7])
@@ -529,19 +565,19 @@
     fin_copy.wait_send()
     ret_copy.wait_send()
 
-    @pl.loop(1, nrow)
+    @pl.loop(0, nrow - 1)
     def _(i):
         codes_copy(i, row).wait_send()
 
-    @pl.loop(1, ncol)
+    @pl.loop(0, ncol - 1)
     def _(i):
         nb_copy(i, col).wait_send()
         miss_copy(i, col).wait_send()
-        msg_copy(i, col).wait_send()
-
-    @pl.loop(1, ncol + 1)
-    def _(i):
-        @pl.when(jnp.logical_or(i < ncol, jnp.logical_not(here)))
+        msg_copy(lax.rem(col + 1 + i, ncol), col).wait_send()
+
+    @pl.loop(0, ncol)
+    def _(i):
+        @pl.when(jnp.logical_or(i < ncol - 1, jnp.logical_not(here)))
         def _():
             att_copy(i).wait_send()
 
@@ -549,7 +585,8 @@
         for d in range(2):
             for h in range(PARTS):
                 hop(t, d, h).wait_send()
-            ret(t, d).wait_send()
+            for h in range(2):
+                ret(t, d, h).wait_send()
 
     if fixed:
         pl.loop(0, steps)(sent)
@@ -580,6 +617,9 @@
     scratch = [
         pltpu.VMEM((count, width), bf),
         pltpu.VMEM((3, width, head_width), bf),
+        pltpu.VMEM((1, count), i32),
+        pltpu.SMEM(block_owner.shape, i32),
+        pltpu.VMEM(neighbours.shape, i32),
         pltpu.VMEM((slots, count), bf),
         pltpu.VMEM((count, slots), bf),
         pltpu.VMEM((8, 128), i32),
@@ -589,8 +629,6 @@
         pltpu.SMEM((8, 128), i32),
         pltpu.VMEM((8, 128), i32),
         pltpu.SMEM((8, 128), i32),
-        pltpu.VMEM((places, PART, half), bf),
-        pltpu.VMEM((places, PART, half), bf),
         pltpu.VMEM((SLOTS_BLK, BLK, half), bf),
         pltpu.VMEM((SLOTS_BLK, BLK, half), bf),
         pltpu.VMEM((PARTS, 2, steps, PART, half), bf),
@@ -609,12 +647,11 @@
         pltpu.SMEM((8, 128), i32),
         pltpu.VMEM((ncol, BLK // 2, 128), bf),
         pltpu.VMEM((ncol, BLK // 2, 128), bf),
-        pltpu.VMEM((2 * steps + 2 * OWN, BLK, hw), bf),
-        pltpu.VMEM((2, steps, BLK, hw), bf),
-        pltpu.VMEM((2, steps, BLK, hw), bf),
+        pltpu.VMEM((2, 2, steps, BLK // 2, hw), bf),
+        pltpu.VMEM((2, 2, steps, BLK // 2, hw), bf),
         pltpu.VMEM((SLOTS_BLK, BLK, hw), bf),
         pltpu.VMEM((SLOTS_BLK, BLK, hw), bf),
-        dma((8,)),
+        dma((11,)),
         dma((nrow,)), dma((nrow,)),
         dma((4,)), dma((4,)),
         dma((PARTS, 2, steps)), dma((PARTS, 2, steps)),
@@ -622,7 +659,9 @@
         dma((ncol,)), dma((ncol,)),
         dma((ncol,)), dma((ncol,)),
         dma((ncol + 1,)), dma((ncol,)),
-        dma((2, steps)), dma((2, steps)),
+        dma((2, 2, steps)), dma((2, 2, steps)),
+        *[pltpu.VMEM((places, PART, half), bf)] * PARTS,
+        *[pltpu.VMEM((2 * steps + 2 * OWN, BLK // 2, hw), bf)] * 2,
     ]
     return pl.pallas_call(
         functools.partial(kernel, (nrow, ncol, heads, width, slot_plan, fixed)),
@@ -630,7 +669,7 @@
             jax.ShapeDtypeStruct((count, head_width), bf),
             jax.ShapeDtypeStruct((1,), i32),
         ),
-        in_specs=[hbm, vmem, smem, vmem, hbm, hbm, hbm],
+        in_specs=[hbm] * 7,
         out_specs=(vmem, smem),
         scratch_shapes=scratch,
         compiler_params=pltpu.CompilerParams(

time: 115 us -> 112 us (0.974)
  Pallas kernels: 113 us -> 109 us
    pallas_call x1, Pallas kernels: 113 us -> 109 us  [routed(): pl.pallas_call(functools.partial(kernel, (nrow, ncol, heads, width, slot_...]
where the time goes in v3:
time: 112 us
  Pallas kernels  109 us (97%)
  local copies, waits for them, and re-layouts  1.5 us (1%)
    pallas_call x1, Pallas kernels, routed(): pl.pallas_call(functools.partial(kernel, (nrow, ncol, heads, width, slot_...  109 us

profile of v3, /device:TPU:1, one launch (start us, length us, event | category | flops | bytes accessed | tf_op | source)
XLA Modules:
  0.0 111.7 jit_solution(8921400030933942163)
XLA Ops:
  0.0 0.0 copy-start.4
  0.0 0.0 copy-start.5
  0.0 0.0 copy-start.6
  0.0 0.7 copy-done.4
  0.7 0.0 copy-done.5
  0.7 0.0 copy-done.6
  0.7 0.0 copy-start
  0.7 0.0 copy-start.1
  0.7 0.0 copy-start.2
  0.7 0.0 copy-start.3
  0.7 109.5 %shard_map.75 = (bf16[512,512]{1,0:T(8,128)(2,1)S(1)}, s32[1]{0:T(128)}) custom-call(bf16[512,1024]{1,0:T(8,128)(2,1)} %tokens_hbm.1, s32[1,512]{1,0:T(1,128)S(1)} %bitcast.3, s32[1,8]{1,0:T(1,128)S(1)} %copy-done.6, s32[2,16]{1,0:T(2,128)S(1)} %copy-done.5, bf16[1024,512]{1,0:T(8,128)(2,1)} %wq_hbm.1, bf16[1024,512]{1,0:T(8,128)(2,1)} %wk_hbm.1, ...), custom_call_target="tpu_custom_call" | custom-call | tf_op jit(solution)/shard_map/pallas_call | solution.py:666
  110.8 0.0 copy-done
  110.8 0.0 copy-done.1
  110.8 0.0 copy-done.2
  110.9 0.0 copy-done.3
  110.9 0.8 copy.13
  (1 shorter events, 0.0 us)
Async XLA Ops:
  0.0 0.7 copy-start.4
  0.0 0.7 copy-start.5
  0.0 0.7 copy-start.6
  0.7 110.1 %copy-start = (bf16[512,1024]{1,0:T(8,128)(2,1)S(1)}, bf16[512,1024]{1,0:T(8,128)(2,1)}, u32[]{:S(2)}) copy-start(bf16[512,1024]{1,0:T(8,128)(2,1)} %tokens_hbm.1) | copy-start | bytes 3145732
  0.7 110.1 %copy-start.1 = (bf16[1024,512]{1,0:T(8,128)(2,1)S(1)}, bf16[1024,512]{1,0:T(8,128)(2,1)}, u32[]{:S(2)}) copy-start(bf16[1024,512]{1,0:T(8,128)(2,1)} %wq_hbm.1) | copy-start | bytes 3145732
  0.7 110.1 %copy-start.2 = (bf16[1024,512]{1,0:T(8,128)(2,1)S(1)}, bf16[1024,512]{1,0:T(8,128)(2,1)}, u32[]{:S(2)}) copy-start(bf16[1024,512]{1,0:T(8,128)(2,1)} %wk_hbm.1) | copy-start | bytes 3145732
  0.7 110.1 %copy-start.3 = (bf16[1024,512]{1,0:T(8,128)(2,1)S(1)}, bf16[1024,512]{1,0:T(8,128)(2,1)}, u32[]{:S(2)}) copy-start(bf16[1024,512]{1,0:T(8,128)(2,1)} %wv_hbm.1) | copy-start | bytes 3145732

commit v4 on v3

--- a/solution.py
+++ b/solution.py
@@ -515,16 +515,56 @@
         for d in range(2):
             ret_stage[h, d, t] = home[h][tbl_s[2, 16 + 2 * t + d]]
             ret(t, d, h).start()
-        if not fixed and s == 1 and h == 0:
-            tell()
+        if not fixed and h == 0:
+            if s == 1:
+                tell()
+            if s == 2:
+                settle()
+            if s == steps - 2:
+                for u in range(steps // 2, steps):
+                    for d in range(2):
+                        for g in range(2):
+                            ret(u, d, g).wait_send()
 
     def tell():
         @pl.loop(0, ncol - 1)
         def _(i):
             miss_copy(i, col).start()
 
+    def settle():
+        code_copy.wait_send()
+        sib_copy.wait_send()
+        fin_copy.wait_send()
+
+        @pl.loop(0, nrow - 1)
+        def _(i):
+            codes_copy(i, row).wait_send()
+
+        @pl.loop(0, ncol - 1)
+        def _(i):
+            nb_copy(i, col).wait_send()
+            msg_copy(lax.rem(col + 1 + i, ncol), col).wait_send()
+
+        @pl.loop(0, ncol)
+        def _(i):
+            @pl.when(jnp.logical_or(i < ncol - 1, jnp.logical_not(here)))
+            def _():
+                att_copy(i).wait_send()
+
+        def sent(t):
+            for d in range(2):
+                for h in range(PARTS):
+                    hop(t, d, h).wait_send()
+
+        if fixed:
+            pl.loop(0, steps)(sent)
+        else:
+            for t in range(steps):
+                sent(t)
+
     if fixed:
         tell()
+        settle()
     ret_needs = [
         steps - min([u for u in range(steps) if needs[u] > t], default=steps)
         for t in reversed(range(steps))
@@ -560,39 +600,22 @@
         hot_t, ret_rx[...].reshape(slots, hw), preferred_element_type=jnp.float32
     ).astype(jnp.bfloat16)
 
-    code_copy.wait_send()
-    sib_copy.wait_send()
-    fin_copy.wait_send()
     ret_copy.wait_send()
 
-    @pl.loop(0, nrow - 1)
-    def _(i):
-        codes_copy(i, row).wait_send()
-
     @pl.loop(0, ncol - 1)
     def _(i):
-        nb_copy(i, col).wait_send()
         miss_copy(i, col).wait_send()
-        msg_copy(lax.rem(col + 1 + i, ncol), col).wait_send()
-
-    @pl.loop(0, ncol)
-    def _(i):
-        @pl.when(jnp.logical_or(i < ncol - 1, jnp.logical_not(here)))
-        def _():
-            att_copy(i).wait_send()
-
-    def sent(t):
+
+    def returned(t):
         for d in range(2):
-            for h in range(PARTS):
-                hop(t, d, h).wait_send()
             for h in range(2):
                 ret(t, d, h).wait_send()
 
     if fixed:
-        pl.loop(0, steps)(sent)
+        pl.loop(0, steps)(returned)
     else:
-        for t in range(steps):
-            sent(t)
+        for t in range(steps // 2):
+            returned(t)
 
 
 def routed(fixed, tokens, merge_map, block_owner, neighbours, w_query, w_key, w_value):

time: 112 us -> 111 us (level)
  no operation moved by 1% of the time
where the time goes in v4:
time: 111 us
  Pallas kernels  109 us (98%)
  local copies, waits for them, and re-layouts  1.5 us (1%)
    pallas_call x1, Pallas kernels, routed(): pl.pallas_call(functools.partial(kernel, (nrow, ncol, heads, width, slot_...  109 us

profile of v4, /device:TPU:1, one launch (start us, length us, event | category | flops | bytes accessed | tf_op | source)
XLA Modules:
  0.0 111.1 jit_solution(13283721163059293750)
XLA Ops:
  0.0 0.0 copy-start.4
  0.0 0.0 copy-start.5
  0.0 0.0 copy-start.6
  0.0 0.7 copy-done.4
  0.7 0.0 copy-done.5
  0.7 0.0 copy-done.6
  0.7 0.0 copy-start
  0.7 0.0 copy-start.1
  0.7 0.0 copy-start.2
  0.7 0.0 copy-start.3
  0.7 108.9 %shard_map.75 = (bf16[512,512]{1,0:T(8,128)(2,1)S(1)}, s32[1]{0:T(128)}) custom-call(bf16[512,1024]{1,0:T(8,128)(2,1)} %tokens_hbm.1, s32[1,512]{1,0:T(1,128)S(1)} %bitcast.3, s32[1,8]{1,0:T(1,128)S(1)} %copy-done.6, s32[2,16]{1,0:T(2,128)S(1)} %copy-done.5, bf16[1024,512]{1,0:T(8,128)(2,1)} %wq_hbm.1, bf16[1024,512]{1,0:T(8,128)(2,1)} %wk_hbm.1, ...), custom_call_target="tpu_custom_call" | custom-call | tf_op jit(solution)/shard_map/pallas_call | solution.py:689
  110.3 0.0 copy-done
  110.3 0.0 copy-done.1
  110.3 0.0 copy-done.2
  110.3 0.0 copy-done.3
  110.3 0.8 copy.13
  (1 shorter events, 0.0 us)
Async XLA Ops:
  0.0 0.7 copy-start.4
  0.0 0.7 copy-start.5
  0.0 0.7 copy-start.6
  0.7 109.6 %copy-start = (bf16[512,1024]{1,0:T(8,128)(2,1)S(1)}, bf16[512,1024]{1,0:T(8,128)(2,1)}, u32[]{:S(2)}) copy-start(bf16[512,1024]{1,0:T(8,128)(2,1)} %tokens_hbm.1) | copy-start | bytes 3145732
  0.7 109.6 %copy-start.1 = (bf16[1024,512]{1,0:T(8,128)(2,1)S(1)}, bf16[1024,512]{1,0:T(8,128)(2,1)}, u32[]{:S(2)}) copy-start(bf16[1024,512]{1,0:T(8,128)(2,1)} %wq_hbm.1) | copy-start | bytes 3145732
  0.7 109.6 %copy-start.2 = (bf16[1024,512]{1,0:T(8,128)(2,1)S(1)}, bf16[1024,512]{1,0:T(8,128)(2,1)}, u32[]{:S(2)}) copy-start(bf16[1024,512]{1,0:T(8,128)(2,1)} %wk_hbm.1) | copy-start | bytes 3145732
  0.7 109.6 %copy-start.3 = (bf16[1024,512]{1,0:T(8,128)(2,1)S(1)}, bf16[1024,512]{1,0:T(8,128)(2,1)}, u32[]{:S(2)}) copy-start(bf16[1024,512]{1,0:T(8,128)(2,1)} %wv_hbm.1) | copy-start | bytes 3145732
